TPU v7x, 32 devices: a whole 2x2x4 slice. The times are simulated.
32 devices in a mesh: ens: 4 (over z), tile: 8 (over y, x, core).
Axes of the slice: x: 2, y: 2, z: 4, core: 2. Of those that a mesh axis runs over, the one named last changes fastest.
Arguments:
- conditioning: bfloat16 [12, 64, 128], P(None, 'tile'), may hold values from -6 to 6
- member_noise: float32 [4, 4, 64, 128], P('ens', None, 'tile'), may hold values from -6 to 6
- reg_in: bfloat16 [3, 3, 12, 128], replicated, may hold values from -1 to 1
- reg_down: bfloat16 [3, 3, 128, 128], replicated, may hold values from -0.25 to 0.25
- reg_low: bfloat16 [3, 3, 128, 128], replicated, may hold values from -0.25 to 0.25
- reg_up: bfloat16 [4, 4, 128, 128], replicated, may hold values from -0.375 to 0.375
- reg_fine: bfloat16 [3, 3, 128, 128], replicated, may hold values from -0.25 to 0.25
- reg_out: bfloat16 [3, 3, 4, 128], replicated, may hold values from -0.3125 to 0.3125
- dif_in: bfloat16 [3, 3, 20, 128], replicated, may hold values from -0.75 to 0.75
- dif_down: bfloat16 [3, 3, 128, 128], replicated, may hold values from -0.25 to 0.25
- dif_low: bfloat16 [3, 3, 128, 128], replicated, may hold values from -0.25 to 0.25
- dif_up: bfloat16 [4, 4, 128, 128], replicated, may hold values from -0.375 to 0.375
- dif_fine: bfloat16 [3, 3, 128, 128], replicated, may hold values from -0.25 to 0.25
- dif_out: bfloat16 [3, 3, 4, 128], replicated, may hold values from -0.3125 to 0.3125
Outputs:
- prediction: float32 [4, 4, 64, 128], P('ens', None, 'tile')
All inputs are finite; a program needn't handle non-finite values.
Results may differ from a plain program's by a relative error of at most 0.015.
Values may be sent and summed in bfloat16 or wider, within the bound.
A program may use at most 64 MiB of HBM per device.

v0:
```python
import jax
import jax.numpy as jnp
from jax import lax
from jax.sharding import PartitionSpec as P

STEPS = 2


sigma_top = 1.0
sigma_ratio = 0.4
sigma_data = 0.5


def with_halo(cells, sides, width):
    for axis, dim in sides:
        count = lax.axis_size(axis)
        ends = count - 1
        head = lax.slice_in_dim(cells, 0, width, axis=dim)
        tail = lax.slice_in_dim(cells, cells.shape[dim] - width, cells.shape[dim], axis=dim)
        cells = jnp.concatenate(
            [
                lax.ppermute(tail, axis, [(i, (i + 1) % count) for i in range(ends)]),
                cells,
                lax.ppermute(head, axis, [((i + 1) % count, i) for i in range(ends)]),
            ],
            axis=dim,
        )
    return cells


def silu_round(values):
    return jax.nn.silu(values).astype(jnp.bfloat16)


def conv_fields(padded, weight):
    height = padded.shape[1] - 2
    across = padded.shape[2] - 2
    running = None
    for tap_y in range(3):
        for tap_x in range(3):
            window = padded[:, tap_y : tap_y + height, tap_x : tap_x + across]
            tap_term = jnp.einsum(
                "crw,co->rwo", window, weight[tap_y, tap_x], preferred_element_type=jnp.float32
            )
            running = tap_term if running is None else running + tap_term
    return running


def conv_feat(padded, weight, stride):
    count_y = (padded.shape[0] - 3) // stride + 1
    count_x = (padded.shape[1] - 3) // stride + 1
    running = None
    for tap_y in range(3):
        for tap_x in range(3):
            window = padded[
                tap_y : tap_y + stride * (count_y - 1) + 1 : stride,
                tap_x : tap_x + stride * (count_x - 1) + 1 : stride,
            ]
            tap_term = jnp.dot(window, weight[tap_y, tap_x], preferred_element_type=jnp.float32)
            running = tap_term if running is None else running + tap_term
    return running


def conv_out(padded, weight):
    height = padded.shape[0] - 2
    across = padded.shape[1] - 2
    running = None
    for tap_y in range(3):
        for tap_x in range(3):
            window = padded[tap_y : tap_y + height, tap_x : tap_x + across]
            tap_term = jnp.einsum(
                "rwc,oc->orw", window, weight[tap_y, tap_x], preferred_element_type=jnp.float32
            )
            running = tap_term if running is None else running + tap_term
    return running


def up_conv(padded, weight):
    count_y = padded.shape[0] - 2
    count_x = padded.shape[1] - 2
    tap_pairs = (((1, 1), (0, 3)), ((2, 0), (1, 2)))

    def parity(side_y, side_x):
        running = None
        for offset_y, kernel_y in tap_pairs[side_y]:
            for offset_x, kernel_x in tap_pairs[side_x]:
                window = padded[offset_y : offset_y + count_y, offset_x : offset_x + count_x]
                tap_term = jnp.dot(
                    window, weight[kernel_y, kernel_x], preferred_element_type=jnp.float32
                )
                running = tap_term if running is None else running + tap_term
        return running

    upper_rows = jnp.stack([parity(0, 0), parity(0, 1)], axis=2)
    lower_rows = jnp.stack([parity(1, 0), parity(1, 1)], axis=2)
    merged = jnp.stack([upper_rows, lower_rows], axis=1)
    return merged.reshape(2 * count_y, 2 * count_x, merged.shape[-1])


def col_pad(values):
    return jnp.pad(values, ((0, 0), (1, 1), (0, 0)))


def feat_pad(values):
    return col_pad(with_halo(values, (("tile", 0),), 1))


def strip_pad(values):
    return with_halo(values, (("ens", 1), ("tile", 0)), 1)


def lower_each(top_level, down_weight, low_weight, up_weight, pad_fn):
    coarse = silu_round(conv_feat(pad_fn(top_level), down_weight, 2))
    middle = silu_round(conv_feat(pad_fn(coarse), low_weight, 1))
    return up_conv(pad_fn(middle), up_weight)


def network_pass(padded_fields, weights, pad_fn, lower_fn):
    in_weight, down_weight, low_weight, up_weight, fine_weight, out_weight = weights
    top_level = silu_round(conv_fields(padded_fields, in_weight))
    upward = lower_fn(top_level, down_weight, low_weight, up_weight, pad_fn)
    summed = (top_level.astype(jnp.float32) + upward).astype(jnp.bfloat16)
    refined = silu_round(conv_feat(pad_fn(summed), fine_weight, 1))
    return conv_out(pad_fn(refined), out_weight)


def shards(
    conditioning,
    member_noise,
    reg_in,
    reg_down,
    reg_low,
    reg_up,
    reg_fine,
    reg_out,
    dif_in,
    dif_down,
    dif_low,
    dif_up,
    dif_fine,
    dif_out,
):
    grid_cols = conditioning.shape[2]
    reg_weights = (reg_in, reg_down, reg_low, reg_up, reg_fine, reg_out)
    dif_weights = (dif_in, dif_down, dif_low, dif_up, dif_fine, dif_out)
    cond_rows = with_halo(conditioning, (("tile", 1),), 1)
    cond_padded = jnp.pad(cond_rows, ((0, 0), (0, 0), (1, 1)))
    strip_width = grid_cols // lax.axis_size("ens")
    strip_start = lax.axis_index("ens") * strip_width
    strip_input = lax.dynamic_slice_in_dim(cond_padded, strip_start, strip_width + 2, 2)
    mean_strip = network_pass(strip_input, reg_weights, strip_pad, lower_each)
    reg_mean = lax.all_gather(mean_strip, "ens", axis=2, tiled=True)
    mean_input = reg_mean.astype(jnp.bfloat16)
    residual_field = sigma_top * member_noise[0]
    for step_index in range(STEPS):
        sigma_now = sigma_top * sigma_ratio**step_index
        sigma_next = sigma_top * sigma_ratio ** (step_index + 1) if step_index + 1 < STEPS else 0.0
        scale_sq = sigma_now**2 + sigma_data**2
        in_gain = 1.0 / scale_sq**0.5
        skip_gain = sigma_data**2 / scale_sq
        out_gain = sigma_now * sigma_data / scale_sq**0.5
        inputs = jnp.concatenate(
            [(in_gain * residual_field).astype(jnp.bfloat16), conditioning, mean_input], axis=0
        )
        inputs_padded = with_halo(inputs, (("tile", 1),), 1)
        inputs_padded = jnp.pad(inputs_padded, ((0, 0), (0, 0), (1, 1)))
        network = network_pass(inputs_padded, dif_weights, feat_pad, lower_each)
        denoised = skip_gain * residual_field + out_gain * network
        residual_field = residual_field + (sigma_next - sigma_now) / sigma_now * (
            residual_field - denoised
        )
    return (reg_mean + residual_field)[None]


def solution(mesh):
    return jax.shard_map(
        shards,
        mesh=mesh,
        in_specs=(
            P(None, "tile", None),
            P("ens", None, "tile", None),
            P(),
            P(),
            P(),
            P(),
            P(),
            P(),
            P(),
            P(),
            P(),
            P(),
            P(),
            P(),
        ),
        out_specs=P("ens", None, "tile", None),
        check_vma=False,
    )
```

profile of v0, /device:TPU:3, one launch (start us, length us, event | category | flops | bytes accessed | tf_op | source)
XLA Modules:
  0.0 243.0 jit_solution(4876951863588240806)
XLA Ops:
  0.8 2.6 %collective-permute-start.1 = (bf16[12,1,128]{2,0,1:T(8,128)(2,1)S(1)}, bf16[12,1,128]{2,0,1:T(8,128)(2,1)S(1)}, u32[]{:S(2)}, u32[]{:S(2)}) collective-permute-start(bf16[12,1,128]{2,0,1:T(8,128)(2,1)S(1)} %get-tuple-element.45), channel_id=1, source_target_pairs={{1,0},{2,1},{3,2},{4,3},{5,4},{6,5},{7,6},{9,8},{10,9},{11,10},{12... | collective-permute-start | bytes 9224 | tf_op jit(solution)/shard_map/ppermute | solution.py:24
  3.3 3.9 %collective-permute-start = (bf16[12,1,128]{2,0,1:T(8,128)(2,1)S(1)}, bf16[12,1,128]{2,0,1:T(8,128)(2,1)S(1)}, u32[]{:S(2)}, u32[]{:S(2)}) collective-permute-start(bf16[12,1,128]{2,0,1:T(8,128)(2,1)S(1)} %get-tuple-element.46), channel_id=1, source_target_pairs={{0,1},{1,2},{2,3},{3,4},{4,5},{5,6},{6,7},{8,9},{9,10},{10,11},{11... | collective-permute-start | bytes 9224 | tf_op jit(solution)/shard_map/ppermute | solution.py:22
  10.7 3.2 %collective-permute-start.2 = (bf16[8,1,128]{2,1,0:T(2,128)(2,1)S(1)}, bf16[8,1,128]{2,1,0:T(2,128)(2,1)S(1)}, u32[]{:S(2)}, u32[]{:S(2)}) collective-permute-start(bf16[8,1,128]{2,1,0:T(2,128)(2,1)S(1)} %get-tuple-element.39), channel_id=1, source_target_pairs={{0,8},{8,16},{16,24},{1,9},{9,17},{17,25},{2,10},{10,18},{18,26},{... | collective-permute-start | bytes 6152 | tf_op jit(solution)/shard_map/ppermute | solution.py:22
  15.8 2.5 %collective-permute-done.3 = bf16[8,1,128]{2,1,0:T(2,128)(2,1)S(1)} collective-permute-done((bf16[8,1,128]{2,1,0:T(2,128)(2,1)S(1)}, bf16[8,1,128]{2,1,0:T(2,128)(2,1)S(1)}, u32[]{:S(2)}, u32[]{:S(2)}) %collective-permute-start.3) | collective-permute-done | bytes 2080 | tf_op jit(solution)/shard_map/ppermute | solution.py:24
  18.4 6.5 %collective-permute-start.4 = (bf16[1,34,128]{2,1,0:T(8,128)(2,1)S(1)}, bf16[1,34,128]{2,1,0:T(8,128)(2,1)S(1)}, u32[]{:S(2)}, u32[]{:S(2)}) collective-permute-start(bf16[1,34,128]{2,1,0:T(8,128)(2,1)S(1)} %get-tuple-element.17), channel_id=1, source_target_pairs={{0,1},{1,2},{2,3},{3,4},{4,5},{5,6},{6,7},{8,9},{9,10},{10,11},{11... | collective-permute-start | bytes 26120 | tf_op jit(solution)/shard_map/ppermute | solution.py:22
  25.0 1.9 collective-permute-start.5
  27.2 3.7 %collective-permute-done.5 = bf16[1,34,128]{2,1,0:T(8,128)(2,1)S(1)} collective-permute-done((bf16[1,34,128]{2,1,0:T(8,128)(2,1)S(1)}, bf16[1,34,128]{2,1,0:T(8,128)(2,1)S(1)}, u32[]{:S(2)}, u32[]{:S(2)}) %collective-permute-start.5) | collective-permute-done | bytes 8736 | tf_op jit(solution)/shard_map/ppermute | solution.py:24
  32.1 3.2 %collective-permute-start.6 = (bf16[4,1,128]{2,1,0:T(2,128)(2,1)S(1)}, bf16[4,1,128]{2,1,0:T(2,128)(2,1)S(1)}, u32[]{:S(2)}, u32[]{:S(2)}) collective-permute-start(bf16[4,1,128]{2,1,0:T(2,128)(2,1)S(1)} %get-tuple-element.57), channel_id=1, source_target_pairs={{0,8},{8,16},{16,24},{1,9},{9,17},{17,25},{2,10},{10,18},{18,26},{... | collective-permute-start | bytes 3080 | tf_op jit(solution)/shard_map/ppermute | solution.py:22
  36.8 2.9 %collective-permute-done.7 = bf16[4,1,128]{2,1,0:T(2,128)(2,1)S(1)} collective-permute-done((bf16[4,1,128]{2,1,0:T(2,128)(2,1)S(1)}, bf16[4,1,128]{2,1,0:T(2,128)(2,1)S(1)}, u32[]{:S(2)}, u32[]{:S(2)}) %collective-permute-start.7) | collective-permute-done | bytes 1056 | tf_op jit(solution)/shard_map/ppermute | solution.py:24
  39.7 3.5 %collective-permute-start.8 = (bf16[1,18,128]{2,1,0:T(8,128)(2,1)S(1)}, bf16[1,18,128]{2,1,0:T(8,128)(2,1)S(1)}, u32[]{:S(2)}, u32[]{:S(2)}) collective-permute-start(bf16[1,18,128]{2,1,0:T(8,128)(2,1)S(1)} %get-tuple-element.53), channel_id=1, source_target_pairs={{0,1},{1,2},{2,3},{3,4},{4,5},{5,6},{6,7},{8,9},{9,10},{10,11},{11... | collective-permute-start | bytes 13832 | tf_op jit(solution)/shard_map/ppermute | solution.py:22
  43.2 1.9 collective-permute-start.9
  45.3 3.8 %collective-permute-done.9 = bf16[1,18,128]{2,1,0:T(8,128)(2,1)S(1)} collective-permute-done((bf16[1,18,128]{2,1,0:T(8,128)(2,1)S(1)}, bf16[1,18,128]{2,1,0:T(8,128)(2,1)S(1)}, u32[]{:S(2)}, u32[]{:S(2)}) %collective-permute-start.9) | collective-permute-done | bytes 4640 | tf_op jit(solution)/shard_map/ppermute | solution.py:24
  50.5 3.2 %collective-permute-start.10 = (bf16[4,1,128]{2,1,0:T(2,128)(2,1)S(1)}, bf16[4,1,128]{2,1,0:T(2,128)(2,1)S(1)}, u32[]{:S(2)}, u32[]{:S(2)}) collective-permute-start(bf16[4,1,128]{2,1,0:T(2,128)(2,1)S(1)} %get-tuple-element.55), channel_id=1, source_target_pairs={{0,8},{8,16},{16,24},{1,9},{9,17},{17,25},{2,10},{10,18},{18,26},{... | collective-permute-start | bytes 3080 | tf_op jit(solution)/shard_map/ppermute | solution.py:22
  55.1 2.9 %collective-permute-done.11 = bf16[4,1,128]{2,1,0:T(2,128)(2,1)S(1)} collective-permute-done((bf16[4,1,128]{2,1,0:T(2,128)(2,1)S(1)}, bf16[4,1,128]{2,1,0:T(2,128)(2,1)S(1)}, u32[]{:S(2)}, u32[]{:S(2)}) %collective-permute-start.11) | collective-permute-done | bytes 1056 | tf_op jit(solution)/shard_map/ppermute | solution.py:24
  58.0 3.4 %collective-permute-start.12 = (bf16[1,18,128]{2,1,0:T(8,128)(2,1)S(1)}, bf16[1,18,128]{2,1,0:T(8,128)(2,1)S(1)}, u32[]{:S(2)}, u32[]{:S(2)}) collective-permute-start(bf16[1,18,128]{2,1,0:T(8,128)(2,1)S(1)} %get-tuple-element.49), channel_id=1, source_target_pairs={{0,1},{1,2},{2,3},{3,4},{4,5},{5,6},{6,7},{8,9},{9,10},{10,11},{11... | collective-permute-start | bytes 13832 | tf_op jit(solution)/shard_map/ppermute | solution.py:22
  61.4 1.9 collective-permute-start.13
  63.6 3.7 %collective-permute-done.13 = bf16[1,18,128]{2,1,0:T(8,128)(2,1)S(1)} collective-permute-done((bf16[1,18,128]{2,1,0:T(8,128)(2,1)S(1)}, bf16[1,18,128]{2,1,0:T(8,128)(2,1)S(1)}, u32[]{:S(2)}, u32[]{:S(2)}) %collective-permute-start.13) | collective-permute-done | bytes 4640 | tf_op jit(solution)/shard_map/ppermute | solution.py:24
  68.8 1.6 collective-permute-start.14
  72.0 2.9 %collective-permute-done.15 = bf16[8,1,128]{2,1,0:T(2,128)(2,1)S(1)} collective-permute-done((bf16[8,1,128]{2,1,0:T(2,128)(2,1)S(1)}, bf16[8,1,128]{2,1,0:T(2,128)(2,1)S(1)}, u32[]{:S(2)}, u32[]{:S(2)}) %collective-permute-start.15) | collective-permute-done | bytes 2080 | tf_op jit(solution)/shard_map/ppermute | solution.py:24
  74.9 3.4 %collective-permute-start.16 = (bf16[1,34,128]{2,1,0:T(8,128)(2,1)S(1)}, bf16[1,34,128]{2,1,0:T(8,128)(2,1)S(1)}, u32[]{:S(2)}, u32[]{:S(2)}) collective-permute-start(bf16[1,34,128]{2,1,0:T(8,128)(2,1)S(1)} %get-tuple-element.25), channel_id=1, source_target_pairs={{0,1},{1,2},{2,3},{3,4},{4,5},{5,6},{6,7},{8,9},{9,10},{10,11},{11... | collective-permute-start | bytes 26120 | tf_op jit(solution)/shard_map/ppermute | solution.py:22
  78.2 1.9 collective-permute-start.17
  80.3 3.8 %collective-permute-done.17 = bf16[1,34,128]{2,1,0:T(8,128)(2,1)S(1)} collective-permute-done((bf16[1,34,128]{2,1,0:T(8,128)(2,1)S(1)}, bf16[1,34,128]{2,1,0:T(8,128)(2,1)S(1)}, u32[]{:S(2)}, u32[]{:S(2)}) %collective-permute-start.17) | collective-permute-done | bytes 8736 | tf_op jit(solution)/shard_map/ppermute | solution.py:24
  85.3 1.6 collective-permute-start.18
  88.5 2.9 %collective-permute-done.19 = bf16[8,1,128]{2,1,0:T(2,128)(2,1)S(1)} collective-permute-done((bf16[8,1,128]{2,1,0:T(2,128)(2,1)S(1)}, bf16[8,1,128]{2,1,0:T(2,128)(2,1)S(1)}, u32[]{:S(2)}, u32[]{:S(2)}) %collective-permute-start.19) | collective-permute-done | bytes 2080 | tf_op jit(solution)/shard_map/ppermute | solution.py:24
  91.4 3.4 %collective-permute-start.20 = (bf16[1,34,128]{2,1,0:T(8,128)(2,1)S(1)}, bf16[1,34,128]{2,1,0:T(8,128)(2,1)S(1)}, u32[]{:S(2)}, u32[]{:S(2)}) collective-permute-start(bf16[1,34,128]{2,1,0:T(8,128)(2,1)S(1)} %get-tuple-element.21), channel_id=1, source_target_pairs={{0,1},{1,2},{2,3},{3,4},{4,5},{5,6},{6,7},{8,9},{9,10},{10,11},{11... | collective-permute-start | bytes 26120 | tf_op jit(solution)/shard_map/ppermute | solution.py:22
  94.7 1.9 collective-permute-start.21
  96.9 3.8 %collective-permute-done.21 = bf16[1,34,128]{2,1,0:T(8,128)(2,1)S(1)} collective-permute-done((bf16[1,34,128]{2,1,0:T(8,128)(2,1)S(1)}, bf16[1,34,128]{2,1,0:T(8,128)(2,1)S(1)}, u32[]{:S(2)}, u32[]{:S(2)}) %collective-permute-start.21) | collective-permute-done | bytes 8736 | tf_op jit(solution)/shard_map/ppermute | solution.py:24
  102.2 12.1 %all_gather.3 = f32[4,8,128]{1,0,2:T(4,128)S(1)} all-gather(f32[4,8,32]{1,0,2:T(4,128)S(1)} %copy.29), channel_id=1, replica_groups=mesh['ens'=4,'tile'=8] {'ens'}, dimensions={2}, use_global_device_ids=true | all-gather | bytes 20480 | tf_op jit(solution)/shard_map/all_gather | solution.py:152
  114.5 3.7 %collective-permute-start.22 = (bf16[20,1,128]{2,0,1:T(8,128)(2,1)S(1)}, bf16[20,1,128]{2,0,1:T(8,128)(2,1)S(1)}, u32[]{:S(2)}, u32[]{:S(2)}) collective-permute-start(bf16[20,1,128]{2,0,1:T(8,128)(2,1)S(1)} %get-tuple-element.43), channel_id=1, source_target_pairs={{0,1},{1,2},{2,3},{3,4},{4,5},{5,6},{6,7},{8,9},{9,10},{10,11},{11... | collective-permute-start | bytes 15368 | tf_op jit(solution)/shard_map/ppermute | solution.py:22
  118.1 2.1 collective-permute-start.23
  120.2 3.9 %collective-permute-done.23 = bf16[20,1,128]{2,0,1:T(8,128)(2,1)S(1)} collective-permute-done((bf16[20,1,128]{2,0,1:T(8,128)(2,1)S(1)}, bf16[20,1,128]{2,0,1:T(8,128)(2,1)S(1)}, u32[]{:S(2)}, u32[]{:S(2)}) %collective-permute-start.23) | collective-permute-done | bytes 5152 | tf_op jit(solution)/shard_map/ppermute | solution.py:24
  127.2 2.0 collective-permute-start.24
  129.2 2.4 collective-permute-start.25
  131.6 3.7 %collective-permute-done.25 = bf16[1,128,128]{2,1,0:T(8,128)(2,1)S(1)} collective-permute-done((bf16[1,128,128]{2,1,0:T(8,128)(2,1)S(1)}, bf16[1,128,128]{2,1,0:T(8,128)(2,1)S(1)}, u32[]{:S(2)}, u32[]{:S(2)}) %collective-permute-start.25) | collective-permute-done | bytes 32800 | tf_op jit(solution)/shard_map/ppermute | solution.py:24
  138.7 1.9 collective-permute-start.26
  140.6 2.4 collective-permute-start.27
  143.0 3.5 %collective-permute-done.27 = bf16[1,64,128]{2,1,0:T(8,128)(2,1)S(1)} collective-permute-done((bf16[1,64,128]{2,1,0:T(8,128)(2,1)S(1)}, bf16[1,64,128]{2,1,0:T(8,128)(2,1)S(1)}, u32[]{:S(2)}, u32[]{:S(2)}) %collective-permute-start.27) | collective-permute-done | bytes 16416 | tf_op jit(solution)/shard_map/ppermute | solution.py:24
  149.2 1.9 collective-permute-start.28
  151.1 2.4 collective-permute-start.29
  153.7 3.4 %collective-permute-done.29 = bf16[1,64,128]{2,1,0:T(8,128)(2,1)S(1)} collective-permute-done((bf16[1,64,128]{2,1,0:T(8,128)(2,1)S(1)}, bf16[1,64,128]{2,1,0:T(8,128)(2,1)S(1)}, u32[]{:S(2)}, u32[]{:S(2)}) %collective-permute-start.29) | collective-permute-done | bytes 16416 | tf_op jit(solution)/shard_map/ppermute | solution.py:24
  159.7 1.9 collective-permute-start.30
  161.7 2.5 %collective-permute-start.31 = (bf16[1,128,128]{2,1,0:T(8,128)(2,1)S(1)}, bf16[1,128,128]{2,1,0:T(8,128)(2,1)S(1)}, u32[]{:S(2)}, u32[]{:S(2)}) collective-permute-start(bf16[1,128,128]{2,1,0:T(8,128)(2,1)S(1)} %get-tuple-element.14), channel_id=1, source_target_pairs={{1,0},{2,1},{3,2},{4,3},{5,4},{6,5},{7,6},{9,8},{10,9},{11,10},{12... | collective-permute-start | bytes 98312 | tf_op jit(solution)/shard_map/ppermute | solution.py:24
  164.2 3.7 %collective-permute-done.31 = bf16[1,128,128]{2,1,0:T(8,128)(2,1)S(1)} collective-permute-done((bf16[1,128,128]{2,1,0:T(8,128)(2,1)S(1)}, bf16[1,128,128]{2,1,0:T(8,128)(2,1)S(1)}, u32[]{:S(2)}, u32[]{:S(2)}) %collective-permute-start.31) | collective-permute-done | bytes 32800 | tf_op jit(solution)/shard_map/ppermute | solution.py:24
  170.1 1.9 collective-permute-start.32
  172.0 2.4 collective-permute-start.33
  174.5 3.7 %collective-permute-done.33 = bf16[1,128,128]{2,1,0:T(8,128)(2,1)S(1)} collective-permute-done((bf16[1,128,128]{2,1,0:T(8,128)(2,1)S(1)}, bf16[1,128,128]{2,1,0:T(8,128)(2,1)S(1)}, u32[]{:S(2)}, u32[]{:S(2)}) %collective-permute-start.33) | collective-permute-done | bytes 32800 | tf_op jit(solution)/shard_map/ppermute | solution.py:24
  180.0 1.9 collective-permute-start.34
  182.0 2.6 %collective-permute-start.35 = (bf16[20,1,128]{2,0,1:T(8,128)(2,1)S(1)}, bf16[20,1,128]{2,0,1:T(8,128)(2,1)S(1)}, u32[]{:S(2)}, u32[]{:S(2)}) collective-permute-start(bf16[20,1,128]{2,0,1:T(8,128)(2,1)S(1)} %get-tuple-element.42), channel_id=1, source_target_pairs={{1,0},{2,1},{3,2},{4,3},{5,4},{6,5},{7,6},{9,8},{10,9},{11,10},{12... | collective-permute-start | bytes 15368 | tf_op jit(solution)/shard_map/ppermute | solution.py:24
  184.6 3.2 %collective-permute-done.35 = bf16[20,1,128]{2,0,1:T(8,128)(2,1)S(1)} collective-permute-done((bf16[20,1,128]{2,0,1:T(8,128)(2,1)S(1)}, bf16[20,1,128]{2,0,1:T(8,128)(2,1)S(1)}, u32[]{:S(2)}, u32[]{:S(2)}) %collective-permute-start.35) | collective-permute-done | bytes 5152 | tf_op jit(solution)/shard_map/ppermute | solution.py:24
  190.9 1.9 collective-permute-start.36
  192.9 2.4 collective-permute-start.37
  195.3 3.7 %collective-permute-done.37 = bf16[1,128,128]{2,1,0:T(8,128)(2,1)S(1)} collective-permute-done((bf16[1,128,128]{2,1,0:T(8,128)(2,1)S(1)}, bf16[1,128,128]{2,1,0:T(8,128)(2,1)S(1)}, u32[]{:S(2)}, u32[]{:S(2)}) %collective-permute-start.37) | collective-permute-done | bytes 32800 | tf_op jit(solution)/shard_map/ppermute | solution.py:24
  202.1 1.9 collective-permute-start.38
  204.0 2.4 collective-permute-start.39
  206.4 3.5 %collective-permute-done.39 = bf16[1,64,128]{2,1,0:T(8,128)(2,1)S(1)} collective-permute-done((bf16[1,64,128]{2,1,0:T(8,128)(2,1)S(1)}, bf16[1,64,128]{2,1,0:T(8,128)(2,1)S(1)}, u32[]{:S(2)}, u32[]{:S(2)}) %collective-permute-start.39) | collective-permute-done | bytes 16416 | tf_op jit(solution)/shard_map/ppermute | solution.py:24
  211.7 1.9 collective-permute-start.40
  213.7 2.4 collective-permute-start.41
  216.2 3.4 %collective-permute-done.41 = bf16[1,64,128]{2,1,0:T(8,128)(2,1)S(1)} collective-permute-done((bf16[1,64,128]{2,1,0:T(8,128)(2,1)S(1)}, bf16[1,64,128]{2,1,0:T(8,128)(2,1)S(1)}, u32[]{:S(2)}, u32[]{:S(2)}) %collective-permute-start.41) | collective-permute-done | bytes 16416 | tf_op jit(solution)/shard_map/ppermute | solution.py:24
  222.2 1.9 collective-permute-start.42
  224.2 2.4 collective-permute-start.43
  226.6 3.7 %collective-permute-done.43 = bf16[1,128,128]{2,1,0:T(8,128)(2,1)S(1)} collective-permute-done((bf16[1,128,128]{2,1,0:T(8,128)(2,1)S(1)}, bf16[1,128,128]{2,1,0:T(8,128)(2,1)S(1)}, u32[]{:S(2)}, u32[]{:S(2)}) %collective-permute-start.43) | collective-permute-done | bytes 32800 | tf_op jit(solution)/shard_map/ppermute | solution.py:24
  232.5 1.9 collective-permute-start.44
  234.4 2.4 collective-permute-start.45
  236.8 3.7 %collective-permute-done.45 = bf16[1,128,128]{2,1,0:T(8,128)(2,1)S(1)} collective-permute-done((bf16[1,128,128]{2,1,0:T(8,128)(2,1)S(1)}, bf16[1,128,128]{2,1,0:T(8,128)(2,1)S(1)}, u32[]{:S(2)}, u32[]{:S(2)}) %collective-permute-start.45) | collective-permute-done | bytes 32800 | tf_op jit(solution)/shard_map/ppermute | solution.py:24
  (329 shorter events, 50.1 us)
Async XLA Ops:
  0.7 6.5 %copy-start.10 = (f32[1,4,8,128]{3,2,1,0:T(8,128)S(1)}, f32[1,4,8,128]{3,2,1,0:T(8,128)}, u32[]{:S(2)}) copy-start(f32[1,4,8,128]{3,2,1,0:T(8,128)} %param.15) | copy-start | bytes 49156
  0.8 6.5 %collective-permute-start.1 = (bf16[12,1,128]{2,0,1:T(8,128)(2,1)S(1)}, bf16[12,1,128]{2,0,1:T(8,128)(2,1)S(1)}, u32[]{:S(2)}, u32[]{:S(2)}) collective-permute-start(bf16[12,1,128]{2,0,1:T(8,128)(2,1)S(1)} %get-tuple-element.45), channel_id=1, source_target_pairs={{1,0},{2,1},{3,2},{4,3},{5,4},{6,5},{7,6},{9,8},{10,9},{11,10},{12... | collective-permute-start | bytes 9224 | tf_op jit(solution)/shard_map/ppermute | solution.py:24
  3.3 4.6 %collective-permute-start = (bf16[12,1,128]{2,0,1:T(8,128)(2,1)S(1)}, bf16[12,1,128]{2,0,1:T(8,128)(2,1)S(1)}, u32[]{:S(2)}, u32[]{:S(2)}) collective-permute-start(bf16[12,1,128]{2,0,1:T(8,128)(2,1)S(1)} %get-tuple-element.46), channel_id=1, source_target_pairs={{0,1},{1,2},{2,3},{3,4},{4,5},{5,6},{6,7},{8,9},{9,10},{10,11},{11... | collective-permute-start | bytes 9224 | tf_op jit(solution)/shard_map/ppermute | solution.py:22
  7.3 0.8 copy-start.9
  10.1 5.2 %copy-start.7 = (bf16[3,3,128,128]{3,2,1,0:T(8,128)(2,1)S(1)}, bf16[3,3,128,128]{3,2,1,0:T(8,128)(2,1)}, u32[]{:S(2)}) copy-start(bf16[3,3,128,128]{3,2,1,0:T(8,128)(2,1)} %param.17) | copy-start | bytes 884740
  10.7 5.1 %collective-permute-start.2 = (bf16[8,1,128]{2,1,0:T(2,128)(2,1)S(1)}, bf16[8,1,128]{2,1,0:T(2,128)(2,1)S(1)}, u32[]{:S(2)}, u32[]{:S(2)}) collective-permute-start(bf16[8,1,128]{2,1,0:T(2,128)(2,1)S(1)} %get-tuple-element.39), channel_id=1, source_target_pairs={{0,8},{8,16},{16,24},{1,9},{9,17},{17,25},{2,10},{10,18},{18,26},{... | collective-permute-start | bytes 6152 | tf_op jit(solution)/shard_map/ppermute | solution.py:22
  13.9 4.4 %collective-permute-start.3 = (bf16[8,1,128]{2,1,0:T(2,128)(2,1)S(1)}, bf16[8,1,128]{2,1,0:T(2,128)(2,1)S(1)}, u32[]{:S(2)}, u32[]{:S(2)}) collective-permute-start(bf16[8,1,128]{2,1,0:T(2,128)(2,1)S(1)} %get-tuple-element.40), channel_id=1, source_target_pairs={{8,0},{16,8},{24,16},{9,1},{17,9},{25,17},{10,2},{18,10},{26,18},{... | collective-permute-start | bytes 6152 | tf_op jit(solution)/shard_map/ppermute | solution.py:24
  18.4 8.7 %collective-permute-start.4 = (bf16[1,34,128]{2,1,0:T(8,128)(2,1)S(1)}, bf16[1,34,128]{2,1,0:T(8,128)(2,1)S(1)}, u32[]{:S(2)}, u32[]{:S(2)}) collective-permute-start(bf16[1,34,128]{2,1,0:T(8,128)(2,1)S(1)} %get-tuple-element.17), channel_id=1, source_target_pairs={{0,1},{1,2},{2,3},{3,4},{4,5},{5,6},{6,7},{8,9},{9,10},{10,11},{11... | collective-permute-start | bytes 26120 | tf_op jit(solution)/shard_map/ppermute | solution.py:22
  25.0 5.9 %collective-permute-start.5 = (bf16[1,34,128]{2,1,0:T(8,128)(2,1)S(1)}, bf16[1,34,128]{2,1,0:T(8,128)(2,1)S(1)}, u32[]{:S(2)}, u32[]{:S(2)}) collective-permute-start(bf16[1,34,128]{2,1,0:T(8,128)(2,1)S(1)} %get-tuple-element.18), channel_id=1, source_target_pairs={{1,0},{2,1},{3,2},{4,3},{5,4},{6,5},{7,6},{9,8},{10,9},{11,10},{12... | collective-permute-start | bytes 26120 | tf_op jit(solution)/shard_map/ppermute | solution.py:24
  31.5 5.1 %copy-start.6 = (bf16[3,3,128,128]{3,2,1,0:T(8,128)(2,1)S(1)}, bf16[3,3,128,128]{3,2,1,0:T(8,128)(2,1)}, u32[]{:S(2)}) copy-start(bf16[3,3,128,128]{3,2,1,0:T(8,128)(2,1)} %param.18) | copy-start | bytes 884740
  32.1 4.7 %collective-permute-start.6 = (bf16[4,1,128]{2,1,0:T(2,128)(2,1)S(1)}, bf16[4,1,128]{2,1,0:T(2,128)(2,1)S(1)}, u32[]{:S(2)}, u32[]{:S(2)}) collective-permute-start(bf16[4,1,128]{2,1,0:T(2,128)(2,1)S(1)} %get-tuple-element.57), channel_id=1, source_target_pairs={{0,8},{8,16},{16,24},{1,9},{9,17},{17,25},{2,10},{10,18},{18,26},{... | collective-permute-start | bytes 3080 | tf_op jit(solution)/shard_map/ppermute | solution.py:22
  35.3 4.3 %collective-permute-start.7 = (bf16[4,1,128]{2,1,0:T(2,128)(2,1)S(1)}, bf16[4,1,128]{2,1,0:T(2,128)(2,1)S(1)}, u32[]{:S(2)}, u32[]{:S(2)}) collective-permute-start(bf16[4,1,128]{2,1,0:T(2,128)(2,1)S(1)} %get-tuple-element.58), channel_id=1, source_target_pairs={{8,0},{16,8},{24,16},{9,1},{17,9},{25,17},{10,2},{18,10},{26,18},{... | collective-permute-start | bytes 3080 | tf_op jit(solution)/shard_map/ppermute | solution.py:24
  39.7 10.4 %copy-start.4 = (bf16[4,4,128,128]{3,2,1,0:T(8,128)(2,1)S(1)}, bf16[4,4,128,128]{3,2,1,0:T(8,128)(2,1)}, u32[]{:S(2)}) copy-start(bf16[4,4,128,128]{3,2,1,0:T(8,128)(2,1)} %param.19) | copy-start | bytes 1572868
  39.7 5.6 %collective-permute-start.8 = (bf16[1,18,128]{2,1,0:T(8,128)(2,1)S(1)}, bf16[1,18,128]{2,1,0:T(8,128)(2,1)S(1)}, u32[]{:S(2)}, u32[]{:S(2)}) collective-permute-start(bf16[1,18,128]{2,1,0:T(8,128)(2,1)S(1)} %get-tuple-element.53), channel_id=1, source_target_pairs={{0,1},{1,2},{2,3},{3,4},{4,5},{5,6},{6,7},{8,9},{9,10},{10,11},{11... | collective-permute-start | bytes 13832 | tf_op jit(solution)/shard_map/ppermute | solution.py:22
  43.2 5.8 %collective-permute-start.9 = (bf16[1,18,128]{2,1,0:T(8,128)(2,1)S(1)}, bf16[1,18,128]{2,1,0:T(8,128)(2,1)S(1)}, u32[]{:S(2)}, u32[]{:S(2)}) collective-permute-start(bf16[1,18,128]{2,1,0:T(8,128)(2,1)S(1)} %get-tuple-element.54), channel_id=1, source_target_pairs={{1,0},{2,1},{3,2},{4,3},{5,4},{6,5},{7,6},{9,8},{10,9},{11,10},{12... | collective-permute-start | bytes 13832 | tf_op jit(solution)/shard_map/ppermute | solution.py:24
  50.5 4.6 %collective-permute-start.10 = (bf16[4,1,128]{2,1,0:T(2,128)(2,1)S(1)}, bf16[4,1,128]{2,1,0:T(2,128)(2,1)S(1)}, u32[]{:S(2)}, u32[]{:S(2)}) collective-permute-start(bf16[4,1,128]{2,1,0:T(2,128)(2,1)S(1)} %get-tuple-element.55), channel_id=1, source_target_pairs={{0,8},{8,16},{16,24},{1,9},{9,17},{17,25},{2,10},{10,18},{18,26},{... | collective-permute-start | bytes 3080 | tf_op jit(solution)/shard_map/ppermute | solution.py:22
  53.7 4.3 %collective-permute-start.11 = (bf16[4,1,128]{2,1,0:T(2,128)(2,1)S(1)}, bf16[4,1,128]{2,1,0:T(2,128)(2,1)S(1)}, u32[]{:S(2)}, u32[]{:S(2)}) collective-permute-start(bf16[4,1,128]{2,1,0:T(2,128)(2,1)S(1)} %get-tuple-element.56), channel_id=1, source_target_pairs={{8,0},{16,8},{24,16},{9,1},{17,9},{25,17},{10,2},{18,10},{26,18},{... | collective-permute-start | bytes 3080 | tf_op jit(solution)/shard_map/ppermute | solution.py:24
  58.0 5.6 %collective-permute-start.12 = (bf16[1,18,128]{2,1,0:T(8,128)(2,1)S(1)}, bf16[1,18,128]{2,1,0:T(8,128)(2,1)S(1)}, u32[]{:S(2)}, u32[]{:S(2)}) collective-permute-start(bf16[1,18,128]{2,1,0:T(8,128)(2,1)S(1)} %get-tuple-element.49), channel_id=1, source_target_pairs={{0,1},{1,2},{2,3},{3,4},{4,5},{5,6},{6,7},{8,9},{9,10},{10,11},{11... | collective-permute-start | bytes 13832 | tf_op jit(solution)/shard_map/ppermute | solution.py:22
  61.4 5.8 %collective-permute-start.13 = (bf16[1,18,128]{2,1,0:T(8,128)(2,1)S(1)}, bf16[1,18,128]{2,1,0:T(8,128)(2,1)S(1)}, u32[]{:S(2)}, u32[]{:S(2)}) collective-permute-start(bf16[1,18,128]{2,1,0:T(8,128)(2,1)S(1)} %get-tuple-element.50), channel_id=1, source_target_pairs={{1,0},{2,1},{3,2},{4,3},{5,4},{6,5},{7,6},{9,8},{10,9},{11,10},{12... | collective-permute-start | bytes 13832 | tf_op jit(solution)/shard_map/ppermute | solution.py:24
  68.7 3.1 %copy-start.5 = (bf16[3,3,128,128]{3,2,1,0:T(8,128)(2,1)S(1)}, bf16[3,3,128,128]{3,2,1,0:T(8,128)(2,1)}, u32[]{:S(2)}) copy-start(bf16[3,3,128,128]{3,2,1,0:T(8,128)(2,1)} %param.20) | copy-start | bytes 884740
  68.8 3.1 %collective-permute-start.14 = (bf16[8,1,128]{2,1,0:T(2,128)(2,1)S(1)}, bf16[8,1,128]{2,1,0:T(2,128)(2,1)S(1)}, u32[]{:S(2)}, u32[]{:S(2)}) collective-permute-start(bf16[8,1,128]{2,1,0:T(2,128)(2,1)S(1)} %get-tuple-element.37), channel_id=1, source_target_pairs={{0,8},{8,16},{16,24},{1,9},{9,17},{17,25},{2,10},{10,18},{18,26},{... | collective-permute-start | bytes 6152 | tf_op jit(solution)/shard_map/ppermute | solution.py:22
  70.5 4.4 %collective-permute-start.15 = (bf16[8,1,128]{2,1,0:T(2,128)(2,1)S(1)}, bf16[8,1,128]{2,1,0:T(2,128)(2,1)S(1)}, u32[]{:S(2)}, u32[]{:S(2)}) collective-permute-start(bf16[8,1,128]{2,1,0:T(2,128)(2,1)S(1)} %get-tuple-element.38), channel_id=1, source_target_pairs={{8,0},{16,8},{24,16},{9,1},{17,9},{25,17},{10,2},{18,10},{26,18},{... | collective-permute-start | bytes 6152 | tf_op jit(solution)/shard_map/ppermute | solution.py:24
  74.9 5.5 %collective-permute-start.16 = (bf16[1,34,128]{2,1,0:T(8,128)(2,1)S(1)}, bf16[1,34,128]{2,1,0:T(8,128)(2,1)S(1)}, u32[]{:S(2)}, u32[]{:S(2)}) collective-permute-start(bf16[1,34,128]{2,1,0:T(8,128)(2,1)S(1)} %get-tuple-element.25), channel_id=1, source_target_pairs={{0,1},{1,2},{2,3},{3,4},{4,5},{5,6},{6,7},{8,9},{9,10},{10,11},{11... | collective-permute-start | bytes 26120 | tf_op jit(solution)/shard_map/ppermute | solution.py:22
  78.2 5.9 %collective-permute-start.17 = (bf16[1,34,128]{2,1,0:T(8,128)(2,1)S(1)}, bf16[1,34,128]{2,1,0:T(8,128)(2,1)S(1)}, u32[]{:S(2)}, u32[]{:S(2)}) collective-permute-start(bf16[1,34,128]{2,1,0:T(8,128)(2,1)S(1)} %get-tuple-element.26), channel_id=1, source_target_pairs={{1,0},{2,1},{3,2},{4,3},{5,4},{6,5},{7,6},{9,8},{10,9},{11,10},{12... | collective-permute-start | bytes 26120 | tf_op jit(solution)/shard_map/ppermute | solution.py:24
  85.3 3.0 %copy-start.11 = (bf16[3,3,4,128]{3,2,1,0:T(4,128)(2,1)S(1)}, bf16[3,3,4,128]{3,2,1,0:T(4,128)(2,1)}, u32[]{:S(2)}) copy-start(bf16[3,3,4,128]{3,2,1,0:T(4,128)(2,1)} %param.21) | copy-start | bytes 27652
  85.3 3.1 %collective-permute-start.18 = (bf16[8,1,128]{2,1,0:T(2,128)(2,1)S(1)}, bf16[8,1,128]{2,1,0:T(2,128)(2,1)S(1)}, u32[]{:S(2)}, u32[]{:S(2)}) collective-permute-start(bf16[8,1,128]{2,1,0:T(2,128)(2,1)S(1)} %get-tuple-element.35), channel_id=1, source_target_pairs={{0,8},{8,16},{16,24},{1,9},{9,17},{17,25},{2,10},{10,18},{18,26},{... | collective-permute-start | bytes 6152 | tf_op jit(solution)/shard_map/ppermute | solution.py:22
  87.0 4.4 %collective-permute-start.19 = (bf16[8,1,128]{2,1,0:T(2,128)(2,1)S(1)}, bf16[8,1,128]{2,1,0:T(2,128)(2,1)S(1)}, u32[]{:S(2)}, u32[]{:S(2)}) collective-permute-start(bf16[8,1,128]{2,1,0:T(2,128)(2,1)S(1)} %get-tuple-element.36), channel_id=1, source_target_pairs={{8,0},{16,8},{24,16},{9,1},{17,9},{25,17},{10,2},{18,10},{26,18},{... | collective-permute-start | bytes 6152 | tf_op jit(solution)/shard_map/ppermute | solution.py:24
  91.4 5.5 %collective-permute-start.20 = (bf16[1,34,128]{2,1,0:T(8,128)(2,1)S(1)}, bf16[1,34,128]{2,1,0:T(8,128)(2,1)S(1)}, u32[]{:S(2)}, u32[]{:S(2)}) collective-permute-start(bf16[1,34,128]{2,1,0:T(8,128)(2,1)S(1)} %get-tuple-element.21), channel_id=1, source_target_pairs={{0,1},{1,2},{2,3},{3,4},{4,5},{5,6},{6,7},{8,9},{9,10},{10,11},{11... | collective-permute-start | bytes 26120 | tf_op jit(solution)/shard_map/ppermute | solution.py:22
  94.7 5.9 %collective-permute-start.21 = (bf16[1,34,128]{2,1,0:T(8,128)(2,1)S(1)}, bf16[1,34,128]{2,1,0:T(8,128)(2,1)S(1)}, u32[]{:S(2)}, u32[]{:S(2)}) collective-permute-start(bf16[1,34,128]{2,1,0:T(8,128)(2,1)S(1)} %get-tuple-element.22), channel_id=1, source_target_pairs={{1,0},{2,1},{3,2},{4,3},{5,4},{6,5},{7,6},{9,8},{10,9},{11,10},{12... | collective-permute-start | bytes 26120 | tf_op jit(solution)/shard_map/ppermute | solution.py:24
  114.5 5.7 %collective-permute-start.22 = (bf16[20,1,128]{2,0,1:T(8,128)(2,1)S(1)}, bf16[20,1,128]{2,0,1:T(8,128)(2,1)S(1)}, u32[]{:S(2)}, u32[]{:S(2)}) collective-permute-start(bf16[20,1,128]{2,0,1:T(8,128)(2,1)S(1)} %get-tuple-element.43), channel_id=1, source_target_pairs={{0,1},{1,2},{2,3},{3,4},{4,5},{5,6},{6,7},{8,9},{9,10},{10,11},{11... | collective-permute-start | bytes 15368 | tf_op jit(solution)/shard_map/ppermute | solution.py:22
  118.1 6.0 %copy-start.8 = (bf16[3,3,20,128]{3,2,1,0:T(8,128)(2,1)S(1)}, bf16[3,3,20,128]{3,2,1,0:T(8,128)(2,1)}, u32[]{:S(2)}) copy-start(bf16[3,3,20,128]{3,2,1,0:T(8,128)(2,1)} %param.22) | copy-start | bytes 138244
  118.1 6.0 %collective-permute-start.23 = (bf16[20,1,128]{2,0,1:T(8,128)(2,1)S(1)}, bf16[20,1,128]{2,0,1:T(8,128)(2,1)S(1)}, u32[]{:S(2)}, u32[]{:S(2)}) collective-permute-start(bf16[20,1,128]{2,0,1:T(8,128)(2,1)S(1)} %get-tuple-element.44), channel_id=1, source_target_pairs={{1,0},{2,1},{3,2},{4,3},{5,4},{6,5},{7,6},{9,8},{10,9},{11,10},{12... | collective-permute-start | bytes 15368 | tf_op jit(solution)/shard_map/ppermute | solution.py:24
  127.2 4.3 %collective-permute-start.24 = (bf16[1,128,128]{2,1,0:T(8,128)(2,1)S(1)}, bf16[1,128,128]{2,1,0:T(8,128)(2,1)S(1)}, u32[]{:S(2)}, u32[]{:S(2)}) collective-permute-start(bf16[1,128,128]{2,1,0:T(8,128)(2,1)S(1)} %get-tuple-element.15), channel_id=1, source_target_pairs={{0,1},{1,2},{2,3},{3,4},{4,5},{5,6},{6,7},{8,9},{9,10},{10,11},{11... | collective-permute-start | bytes 98312 | tf_op jit(solution)/shard_map/ppermute | solution.py:22
  129.2 6.1 %collective-permute-start.25 = (bf16[1,128,128]{2,1,0:T(8,128)(2,1)S(1)}, bf16[1,128,128]{2,1,0:T(8,128)(2,1)S(1)}, u32[]{:S(2)}, u32[]{:S(2)}) collective-permute-start(bf16[1,128,128]{2,1,0:T(8,128)(2,1)S(1)} %get-tuple-element.16), channel_id=1, source_target_pairs={{1,0},{2,1},{3,2},{4,3},{5,4},{6,5},{7,6},{9,8},{10,9},{11,10},{12... | collective-permute-start | bytes 98312 | tf_op jit(solution)/shard_map/ppermute | solution.py:24
  136.3 1.0 copy-start.2
  138.5 8.1 %copy-start.1 = (bf16[3,3,128,128]{3,2,1,0:T(8,128)(2,1)S(1)}, bf16[3,3,128,128]{3,2,1,0:T(8,128)(2,1)}, u32[]{:S(2)}) copy-start(bf16[3,3,128,128]{3,2,1,0:T(8,128)(2,1)} %param.24) | copy-start | bytes 884740
  138.7 4.3 %collective-permute-start.26 = (bf16[1,64,128]{2,1,0:T(8,128)(2,1)S(1)}, bf16[1,64,128]{2,1,0:T(8,128)(2,1)S(1)}, u32[]{:S(2)}, u32[]{:S(2)}) collective-permute-start(bf16[1,64,128]{2,1,0:T(8,128)(2,1)S(1)} %get-tuple-element.33), channel_id=1, source_target_pairs={{0,1},{1,2},{2,3},{3,4},{4,5},{5,6},{6,7},{8,9},{9,10},{10,11},{11... | collective-permute-start | bytes 49160 | tf_op jit(solution)/shard_map/ppermute | solution.py:22
  140.6 6.0 %collective-permute-start.27 = (bf16[1,64,128]{2,1,0:T(8,128)(2,1)S(1)}, bf16[1,64,128]{2,1,0:T(8,128)(2,1)S(1)}, u32[]{:S(2)}, u32[]{:S(2)}) collective-permute-start(bf16[1,64,128]{2,1,0:T(8,128)(2,1)S(1)} %get-tuple-element.34), channel_id=1, source_target_pairs={{1,0},{2,1},{3,2},{4,3},{5,4},{6,5},{7,6},{9,8},{10,9},{11,10},{12... | collective-permute-start | bytes 49160 | tf_op jit(solution)/shard_map/ppermute | solution.py:24
  147.8 1.0 copy-start
  149.2 4.5 %collective-permute-start.28 = (bf16[1,64,128]{2,1,0:T(8,128)(2,1)S(1)}, bf16[1,64,128]{2,1,0:T(8,128)(2,1)S(1)}, u32[]{:S(2)}, u32[]{:S(2)}) collective-permute-start(bf16[1,64,128]{2,1,0:T(8,128)(2,1)S(1)} %get-tuple-element.31), channel_id=1, source_target_pairs={{0,1},{1,2},{2,3},{3,4},{4,5},{5,6},{6,7},{8,9},{9,10},{10,11},{11... | collective-permute-start | bytes 49160 | tf_op jit(solution)/shard_map/ppermute | solution.py:22
  151.1 6.0 %collective-permute-start.29 = (bf16[1,64,128]{2,1,0:T(8,128)(2,1)S(1)}, bf16[1,64,128]{2,1,0:T(8,128)(2,1)S(1)}, u32[]{:S(2)}, u32[]{:S(2)}) collective-permute-start(bf16[1,64,128]{2,1,0:T(8,128)(2,1)S(1)} %get-tuple-element.32), channel_id=1, source_target_pairs={{1,0},{2,1},{3,2},{4,3},{5,4},{6,5},{7,6},{9,8},{10,9},{11,10},{12... | collective-permute-start | bytes 49160 | tf_op jit(solution)/shard_map/ppermute | solution.py:24
  159.7 4.5 %collective-permute-start.30 = (bf16[1,128,128]{2,1,0:T(8,128)(2,1)S(1)}, bf16[1,128,128]{2,1,0:T(8,128)(2,1)S(1)}, u32[]{:S(2)}, u32[]{:S(2)}) collective-permute-start(bf16[1,128,128]{2,1,0:T(8,128)(2,1)S(1)} %get-tuple-element.13), channel_id=1, source_target_pairs={{0,1},{1,2},{2,3},{3,4},{4,5},{5,6},{6,7},{8,9},{9,10},{10,11},{11... | collective-permute-start | bytes 98312 | tf_op jit(solution)/shard_map/ppermute | solution.py:22
  161.7 6.4 %copy-start.3 = (bf16[3,3,128,128]{3,2,1,0:T(8,128)(2,1)S(1)}, bf16[3,3,128,128]{3,2,1,0:T(8,128)(2,1)}, u32[]{:S(2)}) copy-start(bf16[3,3,128,128]{3,2,1,0:T(8,128)(2,1)} %param.26) | copy-start | bytes 884740
  161.7 6.3 %collective-permute-start.31 = (bf16[1,128,128]{2,1,0:T(8,128)(2,1)S(1)}, bf16[1,128,128]{2,1,0:T(8,128)(2,1)S(1)}, u32[]{:S(2)}, u32[]{:S(2)}) collective-permute-start(bf16[1,128,128]{2,1,0:T(8,128)(2,1)S(1)} %get-tuple-element.14), channel_id=1, source_target_pairs={{1,0},{2,1},{3,2},{4,3},{5,4},{6,5},{7,6},{9,8},{10,9},{11,10},{12... | collective-permute-start | bytes 98312 | tf_op jit(solution)/shard_map/ppermute | solution.py:24
  170.1 4.4 %collective-permute-start.32 = (bf16[1,128,128]{2,1,0:T(8,128)(2,1)S(1)}, bf16[1,128,128]{2,1,0:T(8,128)(2,1)S(1)}, u32[]{:S(2)}, u32[]{:S(2)}) collective-permute-start(bf16[1,128,128]{2,1,0:T(8,128)(2,1)S(1)} %get-tuple-element.11), channel_id=1, source_target_pairs={{0,1},{1,2},{2,3},{3,4},{4,5},{5,6},{6,7},{8,9},{9,10},{10,11},{11... | collective-permute-start | bytes 98312 | tf_op jit(solution)/shard_map/ppermute | solution.py:22
  172.0 6.3 %copy-start.12 = (bf16[3,3,4,128]{3,2,1,0:T(4,128)(2,1)S(1)}, bf16[3,3,4,128]{3,2,1,0:T(4,128)(2,1)}, u32[]{:S(2)}) copy-start(bf16[3,3,4,128]{3,2,1,0:T(4,128)(2,1)} %param.27) | copy-start | bytes 27652
  172.0 6.1 %collective-permute-start.33 = (bf16[1,128,128]{2,1,0:T(8,128)(2,1)S(1)}, bf16[1,128,128]{2,1,0:T(8,128)(2,1)S(1)}, u32[]{:S(2)}, u32[]{:S(2)}) collective-permute-start(bf16[1,128,128]{2,1,0:T(8,128)(2,1)S(1)} %get-tuple-element.12), channel_id=1, source_target_pairs={{1,0},{2,1},{3,2},{4,3},{5,4},{6,5},{7,6},{9,8},{10,9},{11,10},{12... | collective-permute-start | bytes 98312 | tf_op jit(solution)/shard_map/ppermute | solution.py:24
  180.0 4.5 %collective-permute-start.34 = (bf16[20,1,128]{2,0,1:T(8,128)(2,1)S(1)}, bf16[20,1,128]{2,0,1:T(8,128)(2,1)S(1)}, u32[]{:S(2)}, u32[]{:S(2)}) collective-permute-start(bf16[20,1,128]{2,0,1:T(8,128)(2,1)S(1)} %get-tuple-element.41), channel_id=1, source_target_pairs={{0,1},{1,2},{2,3},{3,4},{4,5},{5,6},{6,7},{8,9},{9,10},{10,11},{11... | collective-permute-start | bytes 15368 | tf_op jit(solution)/shard_map/ppermute | solution.py:22
  182.0 5.8 %collective-permute-start.35 = (bf16[20,1,128]{2,0,1:T(8,128)(2,1)S(1)}, bf16[20,1,128]{2,0,1:T(8,128)(2,1)S(1)}, u32[]{:S(2)}, u32[]{:S(2)}) collective-permute-start(bf16[20,1,128]{2,0,1:T(8,128)(2,1)S(1)} %get-tuple-element.42), channel_id=1, source_target_pairs={{1,0},{2,1},{3,2},{4,3},{5,4},{6,5},{7,6},{9,8},{10,9},{11,10},{12... | collective-permute-start | bytes 15368 | tf_op jit(solution)/shard_map/ppermute | solution.py:24
  190.9 4.3 %collective-permute-start.36 = (bf16[1,128,128]{2,1,0:T(8,128)(2,1)S(1)}, bf16[1,128,128]{2,1,0:T(8,128)(2,1)S(1)}, u32[]{:S(2)}, u32[]{:S(2)}) collective-permute-start(bf16[1,128,128]{2,1,0:T(8,128)(2,1)S(1)} %get-tuple-element.9), channel_id=1, source_target_pairs={{0,1},{1,2},{2,3},{3,4},{4,5},{5,6},{6,7},{8,9},{9,10},{10,11},{11... | collective-permute-start | bytes 98312 | tf_op jit(solution)/shard_map/ppermute | solution.py:22
  192.9 6.1 %collective-permute-start.37 = (bf16[1,128,128]{2,1,0:T(8,128)(2,1)S(1)}, bf16[1,128,128]{2,1,0:T(8,128)(2,1)S(1)}, u32[]{:S(2)}, u32[]{:S(2)}) collective-permute-start(bf16[1,128,128]{2,1,0:T(8,128)(2,1)S(1)} %get-tuple-element.10), channel_id=1, source_target_pairs={{1,0},{2,1},{3,2},{4,3},{5,4},{6,5},{7,6},{9,8},{10,9},{11,10},{12... | collective-permute-start | bytes 98312 | tf_op jit(solution)/shard_map/ppermute | solution.py:24
  202.1 4.3 %collective-permute-start.38 = (bf16[1,64,128]{2,1,0:T(8,128)(2,1)S(1)}, bf16[1,64,128]{2,1,0:T(8,128)(2,1)S(1)}, u32[]{:S(2)}, u32[]{:S(2)}) collective-permute-start(bf16[1,64,128]{2,1,0:T(8,128)(2,1)S(1)} %get-tuple-element.29), channel_id=1, source_target_pairs={{0,1},{1,2},{2,3},{3,4},{4,5},{5,6},{6,7},{8,9},{9,10},{10,11},{11... | collective-permute-start | bytes 49160 | tf_op jit(solution)/shard_map/ppermute | solution.py:22
  204.0 6.0 %collective-permute-start.39 = (bf16[1,64,128]{2,1,0:T(8,128)(2,1)S(1)}, bf16[1,64,128]{2,1,0:T(8,128)(2,1)S(1)}, u32[]{:S(2)}, u32[]{:S(2)}) collective-permute-start(bf16[1,64,128]{2,1,0:T(8,128)(2,1)S(1)} %get-tuple-element.30), channel_id=1, source_target_pairs={{1,0},{2,1},{3,2},{4,3},{5,4},{6,5},{7,6},{9,8},{10,9},{11,10},{12... | collective-permute-start | bytes 49160 | tf_op jit(solution)/shard_map/ppermute | solution.py:24
  211.7 4.5 %collective-permute-start.40 = (bf16[1,64,128]{2,1,0:T(8,128)(2,1)S(1)}, bf16[1,64,128]{2,1,0:T(8,128)(2,1)S(1)}, u32[]{:S(2)}, u32[]{:S(2)}) collective-permute-start(bf16[1,64,128]{2,1,0:T(8,128)(2,1)S(1)} %get-tuple-element.27), channel_id=1, source_target_pairs={{0,1},{1,2},{2,3},{3,4},{4,5},{5,6},{6,7},{8,9},{9,10},{10,11},{11... | collective-permute-start | bytes 49160 | tf_op jit(solution)/shard_map/ppermute | solution.py:22
  213.7 6.0 %collective-permute-start.41 = (bf16[1,64,128]{2,1,0:T(8,128)(2,1)S(1)}, bf16[1,64,128]{2,1,0:T(8,128)(2,1)S(1)}, u32[]{:S(2)}, u32[]{:S(2)}) collective-permute-start(bf16[1,64,128]{2,1,0:T(8,128)(2,1)S(1)} %get-tuple-element.28), channel_id=1, source_target_pairs={{1,0},{2,1},{3,2},{4,3},{5,4},{6,5},{7,6},{9,8},{10,9},{11,10},{12... | collective-permute-start | bytes 49160 | tf_op jit(solution)/shard_map/ppermute | solution.py:24
  222.2 4.3 %collective-permute-start.42 = (bf16[1,128,128]{2,1,0:T(8,128)(2,1)S(1)}, bf16[1,128,128]{2,1,0:T(8,128)(2,1)S(1)}, u32[]{:S(2)}, u32[]{:S(2)}) collective-permute-start(bf16[1,128,128]{2,1,0:T(8,128)(2,1)S(1)} %get-tuple-element.7), channel_id=1, source_target_pairs={{0,1},{1,2},{2,3},{3,4},{4,5},{5,6},{6,7},{8,9},{9,10},{10,11},{11... | collective-permute-start | bytes 98312 | tf_op jit(solution)/shard_map/ppermute | solution.py:22
  224.2 6.1 %collective-permute-start.43 = (bf16[1,128,128]{2,1,0:T(8,128)(2,1)S(1)}, bf16[1,128,128]{2,1,0:T(8,128)(2,1)S(1)}, u32[]{:S(2)}, u32[]{:S(2)}) collective-permute-start(bf16[1,128,128]{2,1,0:T(8,128)(2,1)S(1)} %get-tuple-element.8), channel_id=1, source_target_pairs={{1,0},{2,1},{3,2},{4,3},{5,4},{6,5},{7,6},{9,8},{10,9},{11,10},{12... | collective-permute-start | bytes 98312 | tf_op jit(solution)/shard_map/ppermute | solution.py:24
  232.5 4.3 %collective-permute-start.44 = (bf16[1,128,128]{2,1,0:T(8,128)(2,1)S(1)}, bf16[1,128,128]{2,1,0:T(8,128)(2,1)S(1)}, u32[]{:S(2)}, u32[]{:S(2)}) collective-permute-start(bf16[1,128,128]{2,1,0:T(8,128)(2,1)S(1)} %get-tuple-element.5), channel_id=1, source_target_pairs={{0,1},{1,2},{2,3},{3,4},{4,5},{5,6},{6,7},{8,9},{9,10},{10,11},{11... | collective-permute-start | bytes 98312 | tf_op jit(solution)/shard_map/ppermute | solution.py:22
  234.4 6.1 %collective-permute-start.45 = (bf16[1,128,128]{2,1,0:T(8,128)(2,1)S(1)}, bf16[1,128,128]{2,1,0:T(8,128)(2,1)S(1)}, u32[]{:S(2)}, u32[]{:S(2)}) collective-permute-start(bf16[1,128,128]{2,1,0:T(8,128)(2,1)S(1)} %get-tuple-element.6), channel_id=1, source_target_pairs={{1,0},{2,1},{3,2},{4,3},{5,4},{6,5},{7,6},{9,8},{10,9},{11,10},{12... | collective-permute-start | bytes 98312 | tf_op jit(solution)/shard_map/ppermute | solution.py:24
where the time goes:
time: 245 us; the launch traced here: 243 us
  starting transfers between devices  109 us (44%)
  waiting for transfers between devices  76.8 us (31%)
  matrix products  33.3 us (14%)
  blocking collectives  12.1 us (5%)
  local copies, waits for them, and re-layouts  7.97 us (3%)
    ppermute x23, waiting for transfers between devices, with_halo(): lax.ppermute(head, axis, [((i + 1) % count, i) for i in range(ends)])  76.1 us
    ppermute x23, starting transfers between devices, with_halo(): lax.ppermute(tail, axis, [(i, (i + 1) % count) for i in range(ends)])  61.8 us
    ppermute x23, starting transfers between devices, with_halo(): lax.ppermute(head, axis, [((i + 1) % count, i) for i in range(ends)])  47.4 us
    dot_general x81, matrix products, conv_feat(): jnp.dot(window, weight[tap_y, tap_x], preferred_element_type=jnp.float32)  13.2 us
    all_gather x1, blocking collectives, shards(): reg_mean = lax.all_gather(mean_strip, 'ens', axis=2, tiled=True)  12.1 us
    dot_general x27, matrix products, conv_fields(): jnp.einsum('crw,co->rwo', window, weight[tap_y, tap_x], preferred_element...  8.26 us
    dot_general x48, matrix products, parity(): jnp.dot(window, weight[kernel_y, kernel_x], preferred_element_type=jnp.fl...  6.77 us
    dot_general x27, matrix products, conv_out(): jnp.einsum('rwc,oc->orw', window, weight[tap_y, tap_x], preferred_element...  5.1 us
  transfers between devices with their start and end apart: 46, of which 23 were waited for; matrix products, arithmetic and copies ran while one was open for 1% of the time, Pallas kernels for 0%

commit v1 on v0

v1 whole, which is shorter than its diff:
```python
import functools

import jax
import jax.numpy as jnp
from jax import lax
from jax.experimental import pallas as pl
from jax.experimental.pallas import tpu as pltpu
from jax.sharding import PartitionSpec as P

STEPS = 2
sigma_top = 1.0
sigma_ratio = 0.4
sigma_data = 0.5

F32 = jnp.float32
BF16 = jnp.bfloat16
HIGH = lax.Precision.HIGHEST
TILE = 8
REACH = 2


def step_gains(k):
    now = sigma_top * sigma_ratio**k
    later = sigma_top * sigma_ratio ** (k + 1) if k + 1 < STEPS else 0.0
    sq = now**2 + sigma_data**2
    return 1.0 / sq**0.5, sigma_data**2 / sq, now * sigma_data / sq**0.5, (later - now) / now


def iota2(shape, dim):
    return lax.broadcasted_iota(jnp.int32, shape, dim)


def one_hot(cond, kind=BF16):
    return jnp.where(cond, 1.0, 0.0).astype(kind)


def silu(v):
    h = 0.5 * v
    return h + h * jnp.tanh(h)


def lane_left(z):
    cols = z.shape[-1]
    half = cols // 2
    lane = iota2(z.shape, 1)
    low = jnp.where(lane == 0, 0.0, pltpu.roll(z, half + 1, 1))
    return jnp.where(lane < half, low, pltpu.roll(z, half, 1))


def lane_right(z):
    cols = z.shape[-1]
    half = cols // 2
    lane = iota2(z.shape, 1)
    high = jnp.where(lane == cols - 1, 0.0, pltpu.roll(z, half - 1, 1))
    return jnp.where(lane < half, pltpu.roll(z, half, 1), high)


def down_one(x):
    return jnp.where(iota2(x.shape, 0) == 0, 0.0, pltpu.roll(x, 1, 0))


def up_one(x):
    n = x.shape[0]
    return jnp.where(iota2(x.shape, 0) == n - 1, 0.0, pltpu.roll(x, n - 1, 0))


def store_fine(ref, row, even, odd):
    half, ch = even.shape
    e, o = even.astype(BF16), odd.astype(BF16)
    ref[row, :half, 0:ch] = down_one(odd).astype(BF16)
    ref[row, half:, 0:ch] = e
    ref[row, :half, ch : 2 * ch] = e
    ref[row, half:, ch : 2 * ch] = o
    ref[row, :half, 2 * ch :] = o
    ref[row, half:, 2 * ch :] = up_one(even).astype(BF16)


def store_coarse(ref, row, v):
    ch = v.shape[1]
    ref[row, :, 0:ch] = down_one(v).astype(BF16)
    ref[row, :, ch : 2 * ch] = v.astype(BF16)
    ref[row, :, 2 * ch :] = up_one(v).astype(BF16)


def dot(a, b):
    return jnp.dot(a, b, preferred_element_type=F32)


def kernel(n, cols, *refs):
    (cond_ref, noise_ref, rin_ref, rdown_h, rlow_h, rup_h, rfine_h, rout_ref,
     din_ref, ddown_h, dlow_h, dup_h, dfine_h, dout_ref, out_ref,
     rdown, rlow, rup, rfine, ddown, dlow, dup, dfine,
     rin, rall, din, dall,
     condb, noiseb, resb, fields, top, coarse, middle, joined, zbuf, mean, res,
     wsem, csend, crecv, nsend, nrecv, rsend, rrecv) = refs
    me = lax.axis_index("tile")
    half = cols // 2
    ch = 128
    loads = [
        pltpu.make_async_copy(src, dst, wsem.at[i])
        for i, (src, dst) in enumerate(
            [(rdown_h, rdown), (rlow_h, rlow), (rup_h, rup), (rfine_h, rfine),
             (ddown_h, ddown), (dlow_h, dlow), (dup_h, dup), (dfine_h, dfine)]
        )
    ]
    offsets = [d for d in range(-REACH, REACH + 1) if d != 0]

    def there(d):
        return (me + d >= 0) & (me + d < n)

    barrier = pltpu.get_barrier_semaphore()
    for d in offsets:
        @pl.when(there(d))
        def _():
            pl.semaphore_signal(barrier, inc=1, device_id={"tile": me + d},
                                device_id_type=pl.DeviceIdType.MESH)
    for copy in loads:
        copy.start()

    perm = one_hot(iota2((cols, cols), 0) == 2 * (iota2((cols, cols), 1) % half) + iota2((cols, cols), 1) // half)
    perm_f = perm.astype(F32)
    nch = cond_ref.shape[0]
    shape = (TILE * 16, nch * TILE)
    m, k = iota2(shape, 0), iota2(shape, 1)
    gather = one_hot(k == (m % 16) * TILE + m // 16)
    gather = jnp.where(m % 16 < nch, gather.astype(F32), 0.0).astype(BF16)
    own = cond_ref[...].astype(F32).reshape(nch * TILE, cols).astype(BF16)
    own = dot(gather, dot(own, perm).astype(BF16)).astype(BF16)
    condb[REACH] = own.reshape(TILE, 16, cols)
    shape = (TILE * 8, 4 * TILE)
    m, k = iota2(shape, 0), iota2(shape, 1)
    pick = jnp.where((m % 8 < 4) & (k == (m % 8) * TILE + m // 8), 1.0, 0.0)
    noise = noise_ref[...].reshape(4 * TILE, cols)
    noise = jnp.dot(noise, perm_f, precision=HIGH, preferred_element_type=F32)
    noise = sigma_top * jnp.dot(pick, noise, precision=HIGH, preferred_element_type=F32)
    res[...] = noise
    noiseb[1] = (step_gains(0)[0] * noise).astype(BF16)
    for d in offsets:
        @pl.when(jnp.logical_not(there(d)))
        def _():
            condb[REACH + d] = jnp.zeros_like(condb[REACH + d])
            if abs(d) == 1:
                noiseb[1 + d] = jnp.zeros_like(noiseb[1 + d])
                resb[1 + d] = jnp.zeros_like(resb[1 + d])

    pl.semaphore_wait(barrier, jnp.minimum(me, REACH) + jnp.minimum(n - 1 - me, REACH))

    def cond_copy(d, incoming=False):
        return pltpu.make_async_remote_copy(
            src_ref=condb.at[REACH], dst_ref=condb.at[REACH + (d if incoming else -d)],
            send_sem=csend.at[REACH + d], recv_sem=crecv.at[REACH + (d if incoming else -d)],
            device_id={"tile": me + d}, device_id_type=pl.DeviceIdType.MESH)

    def side_copy(buf, send, recv, d, incoming=False):
        return pltpu.make_async_remote_copy(
            src_ref=buf.at[1], dst_ref=buf.at[1 + (d if incoming else -d)],
            send_sem=send.at[1 + d], recv_sem=recv.at[1 + (d if incoming else -d)],
            device_id={"tile": me + d}, device_id_type=pl.DeviceIdType.MESH)

    for d in offsets:
        @pl.when(there(d))
        def _():
            cond_copy(d).start()
    for d in (-1, 1):
        @pl.when(there(d))
        def _():
            side_copy(noiseb, nsend, nrecv, d).start()

    def place_in(src, dst, cin):
        sh = (24, cin)
        a, b = iota2(sh, 0), iota2(sh, 1)
        if cin == nch:
            take = one_hot(a == b + 8)
        else:
            want = jnp.where(b < 4, b, jnp.where(b < 4 + nch, b + 4, b - nch))
            take = one_hot(a == want)
        for y in range(3):
            parts = [dot(take, src[y, x]) for x in range(3)]
            parts.append(jnp.zeros((8, ch), F32))
            dst[y * 80 : (y + 1) * 80] = jnp.concatenate(parts, axis=0).astype(BF16)

    def place_out(src, dst, at):
        take = one_hot(iota2((8, 4), 0) == iota2((8, 4), 1) + at)
        parts = [dot(take, src[y, x]) for y in range(3) for x in range(3)]
        parts.append(jnp.zeros((8, ch), F32))
        dst[...] = jnp.concatenate(parts, axis=0).astype(BF16)

    place_in(rin_ref, rin, nch)
    place_out(rout_ref, rall, 4)
    place_in(din_ref, din, nch + 8)
    place_out(dout_ref, dall, 0)

    def put_fields(d, eight):
        wide = jnp.concatenate([eight, condb[REACH + d].astype(F32)], axis=1)
        flat = wide.reshape(TILE * 24, cols)
        left = lane_left(flat).reshape(TILE, 24, cols)
        right = lane_right(flat).reshape(TILE, 24, cols)
        both = jnp.concatenate(
            [left, wide, right, jnp.zeros((TILE, 8, cols), F32)], axis=1).astype(BF16)
        at = (REACH + d) * TILE
        fields[at : at + TILE] = both

    def unet(lo, hi, w_in, w_down, w_low, w_up, w_fine, w_all, waits):
        span = hi - lo
        first = me * TILE
        last = n * TILE

        def keep(v, g):
            return jnp.where((g + first >= 0) & (g + first < last), v, 0.0)

        def loop(count, chunk, body):
            def step(i, c):
                body(i * chunk)
                return c
            assert count % chunk == 0
            lax.fori_loop(0, count // chunk, step, 0)

        def do_top(r0):
            c = 2
            parts = []
            for i in range(c):
                parts.append(jnp.concatenate(
                    [fields[r0 + (i + y + lo + 8)] for y in range(3)], axis=0))
            lhs = jnp.concatenate(parts, axis=1)
            v = silu(lax.dot_general(lhs, w_in[...], (((0,), (0,)), ((), ())),
                                     preferred_element_type=F32))
            for i in range(c):
                u = keep(v[i * cols : (i + 1) * cols], r0 + (i + lo - 7))
                store_fine(top, r0 + i, u[:half], u[half:])

        loop(span + 14, 2, do_top)
        waits[0]()

        def do_coarse(r0):
            c = 2
            lhs = jnp.concatenate(
                [jnp.concatenate([top[2 * r0 + 2 * i + y, :half, :] for y in range(3)], axis=1)
                 for i in range(c)], axis=0)
            v = silu(dot(lhs, w_down[...]))
            for i in range(c):
                u = keep(v[i * half : (i + 1) * half], 2 * r0 + (2 * i + lo - 6))
                store_coarse(coarse, r0 + i, u)

        loop(span // 2 + 6, 2, do_coarse)
        waits[1]()

        def do_middle(r0):
            c = 4
            lhs = jnp.concatenate(
                [coarse[pl.ds(r0 + y, c)].reshape(c * half, 3 * ch) for y in range(3)], axis=1)
            v = silu(dot(lhs, w_low[...]))
            for i in range(c):
                u = keep(v[i * half : (i + 1) * half], 2 * r0 + (2 * i + lo - 4))
                store_coarse(middle, r0 + i, u)

        loop(span // 2 + 4, 4, do_middle)
        waits[2]()

        def do_joined(p0):
            c = 2
            rows = [middle[pl.ds(p0 + y, c)].reshape(c * half, 3 * ch) for y in range(3)]
            for ry, ((a, ka), (b, kb)) in enumerate((((0, 3), (1, 1)), ((1, 2), (2, 0)))):
                sums = []
                for at, kx in ((0, (3, 1)), (ch, (2, 0))):
                    lhs = jnp.concatenate(
                        [rows[a][:, at : at + 2 * ch], rows[b][:, at : at + 2 * ch]], axis=1)
                    rhs = jnp.concatenate(
                        [w_up[4 * ky + x] for ky in (ka, kb) for x in kx], axis=0)
                    sums.append(dot(lhs, rhs))
                for i in range(c):
                    t = 2 * p0 + (2 * i + ry)
                    g = t + (lo - 2)
                    base = top[t + 5, :, ch : 2 * ch].astype(F32)
                    even = keep(base[:half] + sums[0][i * half : (i + 1) * half], g)
                    odd = keep(base[half:] + sums[1][i * half : (i + 1) * half], g)
                    store_fine(joined, t, even, odd)

        loop(span // 2 + 2, 2, do_joined)
        waits[3]()

        def do_refined(r0):
            c = 2
            lhs = jnp.concatenate(
                [joined[pl.ds(r0 + y, c)].reshape(c * cols, 3 * ch) for y in range(3)], axis=1)
            v = silu(dot(lhs, w_fine[...]))
            for i in range(c):
                u = keep(v[i * cols : (i + 1) * cols], r0 + (i + lo - 1)).astype(BF16)
                zbuf[r0 + i] = lax.dot_general(
                    w_all[...], u, (((1,), (1,)), ((), ())), preferred_element_type=F32)

        loop(span + 2, 2, do_refined)
        sums = []
        for x in range(3):
            acc = None
            for y in range(3):
                s = 8 * (3 * y + x)
                term = zbuf[y : y + span, s : s + 8, :]
                acc = term if acc is None else acc + term
            sums.append(acc.reshape(span * 8, cols))
        return lane_left(sums[0]) + sums[1] + lane_right(sums[2])

    for d in offsets:
        @pl.when(there(d))
        def _():
            cond_copy(d, True).wait_recv()
    for d in range(-REACH, REACH + 1):
        put_fields(d, jnp.zeros((TILE, 8, cols), F32))
    value = unet(-TILE, 2 * TILE, rin, rdown, rlow, rup, rfine, rall,
                 [c.wait for c in loads[:4]])
    for d in (-1, 0, 1):
        part = value[(d + 1) * 64 : (d + 2) * 64]
        mean[d + 1] = jnp.where(there(d), part, 0.0)

    nothing = lambda: None
    for step in range(STEPS):
        buf, send, recv = (noiseb, nsend, nrecv) if step == 0 else (resb, rsend, rrecv)
        in_gain, skip, gain, rate = step_gains(step)
        for d in (-1, 1):
            @pl.when(there(d))
            def _():
                side_copy(buf, send, recv, d, True).wait_recv()
        for d in (-1, 0, 1):
            put_fields(d, (buf[1 + d].astype(F32) + mean[1 + d]).reshape(TILE, 8, cols))
        net = unet(0, TILE, din, ddown, dlow, dup, dfine, dall,
                   [c.wait for c in loads[4:]] if step == 0 else [nothing] * 4)
        now = res[...]
        now = now + rate * (now - (skip * now + gain * net))
        if step + 1 < STEPS:
            res[...] = now
            resb[1] = (step_gains(step + 1)[0] * now).astype(BF16)
            for d in (-1, 1):
                @pl.when(there(d))
                def _():
                    side_copy(resb, rsend, rrecv, d).start()

    total = now + mean[1]
    shape = (4 * TILE, TILE * 8)
    m, k = iota2(shape, 0), iota2(shape, 1)
    back = jnp.where((k % 4 == m // TILE) & (k // 8 == m % TILE), 1.0, 0.0)
    total = jnp.dot(back, total, precision=HIGH, preferred_element_type=F32)
    total = lax.dot_general(total, perm_f, (((1,), (1,)), ((), ())), precision=HIGH,
                            preferred_element_type=F32)
    out_ref[...] = total.reshape(1, 4, TILE, cols)

    for d in offsets:
        @pl.when(there(d))
        def _():
            cond_copy(d).wait_send()
    for d in (-1, 1):
        @pl.when(there(d))
        def _():
            side_copy(noiseb, nsend, nrecv, d).wait_send()
            side_copy(resb, rsend, rrecv, d).wait_send()


def shards(cond, noise, rin, rdown, rlow, rup, rfine, rout, din, ddown, dlow, dup, dfine, dout):
    n = lax.axis_size("tile")
    cols = cond.shape[2]
    half = cols // 2
    ch = rdown.shape[-1]
    flat = lambda w: w.reshape(-1, ch)
    taps = lambda w: w.reshape(16, ch, ch)
    vm = pl.BlockSpec(memory_space=pltpu.VMEM)
    hb = pl.BlockSpec(memory_space=pl.ANY)
    big = (9 * ch, ch)
    wide = 3 * TILE
    dma = pltpu.SemaphoreType.DMA
    return pl.pallas_call(
        functools.partial(kernel, n, cols),
        out_shape=jax.ShapeDtypeStruct(noise.shape, F32),
        in_specs=[vm, vm, vm, hb, hb, hb, hb, vm, vm, hb, hb, hb, hb, vm],
        out_specs=vm,
        scratch_shapes=[
            *[pltpu.VMEM(s, BF16) for s in (big, big, (16, ch, ch), big) * 2],
            pltpu.VMEM((240, ch), BF16),
            pltpu.VMEM((80, ch), BF16),
            pltpu.VMEM((240, ch), BF16),
            pltpu.VMEM((80, ch), BF16),
            pltpu.VMEM((2 * REACH + 1, TILE, 16, cols), BF16),
            pltpu.VMEM((3, TILE * 8, cols), BF16),
            pltpu.VMEM((3, TILE * 8, cols), BF16),
            pltpu.VMEM((5 * TILE, 80, cols), BF16),
            pltpu.VMEM((wide + 14, cols, 3 * ch), BF16),
            pltpu.VMEM((wide // 2 + 6, half, 3 * ch), BF16),
            pltpu.VMEM((wide // 2 + 4, half, 3 * ch), BF16),
            pltpu.VMEM((wide + 4, cols, 3 * ch), BF16),
            pltpu.VMEM((wide + 2, 80, cols), F32),
            pltpu.VMEM((3, TILE * 8, cols), F32),
            pltpu.VMEM((TILE * 8, cols), F32),
            dma((8,)), dma((5,)), dma((5,)), dma((3,)), dma((3,)), dma((3,)), dma((3,)),
        ],
        compiler_params=pltpu.CompilerParams(
            collective_id=0, has_side_effects=True, vmem_limit_bytes=48 * 1024 * 1024
        ),
        cost_estimate=pl.CostEstimate(flops=4 * 10**9, bytes_accessed=3 * 10**6, transcendentals=2 * 10**6),
    )(cond, noise, rin, flat(rdown), flat(rlow), taps(rup), flat(rfine), rout,
      din, flat(ddown), flat(dlow), taps(dup), flat(dfine), dout)


def solution(mesh):
    return jax.shard_map(
        shards,
        mesh=mesh,
        in_specs=(P(None, "tile", None), P("ens", None, "tile", None)) + (P(),) * 12,
        out_specs=P("ens", None, "tile", None),
        check_vma=False,
    )
```

time: 245 us -> 57.2 us (0.23)
  starting transfers between devices: 109 us -> 0 us
  waiting for transfers between devices: 76.8 us -> 0 us
  Pallas kernels: 0 us -> 43.6 us
  matrix products: 33.3 us -> 0 us
  blocking collectives: 12.1 us -> 0 us
  local copies, waits for them, and re-layouts: 7.97 us -> 12.9 us
    ppermute x46 -> x0, starting transfers between devices: 109 us -> none  [the longest x23 61.8 us: with_halo(): lax.ppermute(tail, axis, [(i, (i + 1) % count) for i in range(ends)])]
    ppermute x46 -> x0, waiting for transfers between devices: 76.8 us -> none  [the longest x23 76.1 us: with_halo(): lax.ppermute(head, axis, [((i + 1) % count, i) for i in range(ends)])]
    pallas_call x0 -> x1, Pallas kernels: none -> 43.6 us  [shards(): pl.pallas_call(functools.partial(kernel, n, cols), out_shape=jax.ShapeDty...]
    dot_general x183 -> x0, matrix products: 33.3 us -> none  [the longest x81 13.2 us: conv_feat(): jnp.dot(window, weight[tap_y, tap_x], preferred_element_type=jnp.float32)]
    all_gather x1 -> x0, blocking collectives: 12.1 us -> none  [shards(): reg_mean = lax.all_gather(mean_strip, 'ens', axis=2, tiled=True)]
    unnamed x27 -> x29, local copies, waits for them, and re-layouts: 1.9 us -> 12.9 us
    slice x46 -> x0, local copies, waits for them, and re-layouts: 4.33 us -> none  [the longest x27 4.21 us: conv_feat(): padded[tap_y:tap_y + stride * (count_y - 1) + 1:stride, tap_x:tap_x + str...]
  transfers between devices with their start and end apart: 46 -> 0, of which waited for: 23 -> 0; matrix products, arithmetic and copies ran while one was open for 1% -> 0% of each run, Pallas kernels for 0% -> 0%
where the time goes in v1:
time: 57.2 us; the launch traced here: 56.5 us
  Pallas kernels  43.6 us (76%)
  local copies, waits for them, and re-layouts  12.9 us (23%)
    pallas_call x1, Pallas kernels, shards(): pl.pallas_call(functools.partial(kernel, n, cols), out_shape=jax.ShapeDty...  43.6 us
    unnamed x29, local copies, waits for them, and re-layouts  12.9 us

profile of v1, /device:TPU:3, one launch (start us, length us, event | category | flops | bytes accessed | tf_op | source)
XLA Modules:
  0.0 56.5 jit_solution(16907841229638930935)
XLA Ops:
  0.0 0.0 copy-start.12
  0.0 0.7 %copy-done.12 = bf16[3,3,4,128]{3,2,1,0:T(4,128)(2,1)S(1)} copy-done((bf16[3,3,4,128]{3,2,1,0:T(4,128)(2,1)S(1)}, bf16[3,3,4,128]{3,2,1,0:T(4,128)(2,1)}, u32[]{:S(2)}) %copy-start.12) | copy-done | bytes 9240
  0.7 0.0 copy-start
  0.7 1.0 %copy-done = bf16[4,4,128,128]{3,2,1,0:T(8,128)(2,1)S(1)} copy-done((bf16[4,4,128,128]{3,2,1,0:T(8,128)(2,1)S(1)}, bf16[4,4,128,128]{3,2,1,0:T(8,128)(2,1)}, u32[]{:S(2)}) %copy-start) | copy-done | bytes 524312
  1.7 0.0 copy-start.1
  1.7 1.0 %copy-done.1 = bf16[4,4,128,128]{3,2,1,0:T(8,128)(2,1)S(1)} copy-done((bf16[4,4,128,128]{3,2,1,0:T(8,128)(2,1)S(1)}, bf16[4,4,128,128]{3,2,1,0:T(8,128)(2,1)}, u32[]{:S(2)}) %copy-start.1) | copy-done | bytes 524312
  2.8 0.0 copy-start.2
  2.8 1.0 %copy-done.2 = bf16[3,3,128,128]{3,2,1,0:T(8,128)(2,1)S(1)} copy-done((bf16[3,3,128,128]{3,2,1,0:T(8,128)(2,1)S(1)}, bf16[3,3,128,128]{3,2,1,0:T(8,128)(2,1)}, u32[]{:S(2)}) %copy-start.2) | copy-done | bytes 294936
  3.7 0.0 copy-start.3
  3.7 1.0 %copy-done.3 = bf16[3,3,128,128]{3,2,1,0:T(8,128)(2,1)S(1)} copy-done((bf16[3,3,128,128]{3,2,1,0:T(8,128)(2,1)S(1)}, bf16[3,3,128,128]{3,2,1,0:T(8,128)(2,1)}, u32[]{:S(2)}) %copy-start.3) | copy-done | bytes 294936
  4.7 0.0 copy-start.4
  4.7 1.0 %copy-done.4 = bf16[3,3,128,128]{3,2,1,0:T(8,128)(2,1)S(1)} copy-done((bf16[3,3,128,128]{3,2,1,0:T(8,128)(2,1)S(1)}, bf16[3,3,128,128]{3,2,1,0:T(8,128)(2,1)}, u32[]{:S(2)}) %copy-start.4) | copy-done | bytes 294936
  5.7 0.0 copy-start.5
  5.7 1.0 %copy-done.5 = bf16[3,3,128,128]{3,2,1,0:T(8,128)(2,1)S(1)} copy-done((bf16[3,3,128,128]{3,2,1,0:T(8,128)(2,1)S(1)}, bf16[3,3,128,128]{3,2,1,0:T(8,128)(2,1)}, u32[]{:S(2)}) %copy-start.5) | copy-done | bytes 294936
  6.6 0.0 copy-start.6
  6.6 1.0 %copy-done.6 = bf16[3,3,128,128]{3,2,1,0:T(8,128)(2,1)S(1)} copy-done((bf16[3,3,128,128]{3,2,1,0:T(8,128)(2,1)S(1)}, bf16[3,3,128,128]{3,2,1,0:T(8,128)(2,1)}, u32[]{:S(2)}) %copy-start.6) | copy-done | bytes 294936
  7.6 0.0 copy-start.7
  7.6 1.0 %copy-done.7 = bf16[3,3,128,128]{3,2,1,0:T(8,128)(2,1)S(1)} copy-done((bf16[3,3,128,128]{3,2,1,0:T(8,128)(2,1)S(1)}, bf16[3,3,128,128]{3,2,1,0:T(8,128)(2,1)}, u32[]{:S(2)}) %copy-start.7) | copy-done | bytes 294936
  8.6 0.0 copy-start.8
  8.6 0.8 %copy-done.8 = bf16[3,3,20,128]{3,2,1,0:T(8,128)(2,1)S(1)} copy-done((bf16[3,3,20,128]{3,2,1,0:T(8,128)(2,1)S(1)}, bf16[3,3,20,128]{3,2,1,0:T(8,128)(2,1)}, u32[]{:S(2)}) %copy-start.8) | copy-done | bytes 46104
  9.4 0.0 copy-start.9
  9.4 0.8 %copy-done.9 = bf16[3,3,12,128]{3,2,1,0:T(8,128)(2,1)S(1)} copy-done((bf16[3,3,12,128]{3,2,1,0:T(8,128)(2,1)S(1)}, bf16[3,3,12,128]{3,2,1,0:T(8,128)(2,1)}, u32[]{:S(2)}) %copy-start.9) | copy-done | bytes 27672
  10.1 0.0 copy-start.10
  10.1 0.7 %copy-done.10 = bf16[12,8,128]{2,1,0:T(8,128)(2,1)S(1)} copy-done((bf16[12,8,128]{2,1,0:T(8,128)(2,1)S(1)}, bf16[12,8,128]{2,1,0:T(8,128)(2,1)}, u32[]{:S(2)}) %copy-start.10) | copy-done | bytes 24600
  10.9 0.0 copy-start.11
  10.9 0.7 %copy-done.11 = f32[1,4,8,128]{3,2,1,0:T(8,128)S(1)} copy-done((f32[1,4,8,128]{3,2,1,0:T(8,128)S(1)}, f32[1,4,8,128]{3,2,1,0:T(8,128)}, u32[]{:S(2)}) %copy-start.11) | copy-done | bytes 16408
  11.6 0.0 copy-start.13
  11.6 0.7 %copy-done.13 = bf16[3,3,4,128]{3,2,1,0:T(4,128)(2,1)S(1)} copy-done((bf16[3,3,4,128]{3,2,1,0:T(4,128)(2,1)S(1)}, bf16[3,3,4,128]{3,2,1,0:T(4,128)(2,1)}, u32[]{:S(2)}) %copy-start.13) | copy-done | bytes 9240
  12.3 43.6 %shard_map.136 = f32[1,4,8,128]{3,2,1,0:T(8,128)S(1)} custom-call(bf16[12,8,128]{2,1,0:T(8,128)(2,1)S(1)} %copy-done.10, f32[1,4,8,128]{3,2,1,0:T(8,128)S(1)} %copy-done.11, bf16[3,3,12,128]{3,2,1,0:T(8,128)(2,1)S(1)} %copy-done.9, bf16[1152,128]{1,0:T(8,128)(2,1)S(1)} %bitcast.10, bf16[1152,128]{1,0:T(8,128)(2,1)S(1)} %bitcast.11, ...), custom_call_target="tpu_custom_call" | custom-call | flops 4000000000 | bytes 3000000 | tf_op jit(solution)/shard_map/pallas_call | solution.py:368
  55.9 0.6 %copy.16 = f32[1,4,8,128]{3,2,1,0:T(8,128)} copy(f32[1,4,8,128]{3,2,1,0:T(8,128)S(1)} %shard_map.136) | data formatting | bytes 32768
Async XLA Ops:
  0.0 0.7 %copy-start.12 = (bf16[3,3,4,128]{3,2,1,0:T(4,128)(2,1)S(1)}, bf16[3,3,4,128]{3,2,1,0:T(4,128)(2,1)}, u32[]{:S(2)}) copy-start(bf16[3,3,4,128]{3,2,1,0:T(4,128)(2,1)} %refs_7_.1) | copy-start | bytes 27652
  0.7 1.0 %copy-start = (bf16[4,4,128,128]{3,2,1,0:T(8,128)(2,1)S(1)}, bf16[4,4,128,128]{3,2,1,0:T(8,128)(2,1)}, u32[]{:S(2)}) copy-start(bf16[4,4,128,128]{3,2,1,0:T(8,128)(2,1)} %param.19) | copy-start | bytes 1572868
  1.7 1.0 %copy-start.1 = (bf16[4,4,128,128]{3,2,1,0:T(8,128)(2,1)S(1)}, bf16[4,4,128,128]{3,2,1,0:T(8,128)(2,1)}, u32[]{:S(2)}) copy-start(bf16[4,4,128,128]{3,2,1,0:T(8,128)(2,1)} %param.25) | copy-start | bytes 1572868
  2.8 1.0 %copy-start.2 = (bf16[3,3,128,128]{3,2,1,0:T(8,128)(2,1)S(1)}, bf16[3,3,128,128]{3,2,1,0:T(8,128)(2,1)}, u32[]{:S(2)}) copy-start(bf16[3,3,128,128]{3,2,1,0:T(8,128)(2,1)} %param.17) | copy-start | bytes 884740
  3.7 1.0 %copy-start.3 = (bf16[3,3,128,128]{3,2,1,0:T(8,128)(2,1)S(1)}, bf16[3,3,128,128]{3,2,1,0:T(8,128)(2,1)}, u32[]{:S(2)}) copy-start(bf16[3,3,128,128]{3,2,1,0:T(8,128)(2,1)} %param.18) | copy-start | bytes 884740
  4.7 1.0 %copy-start.4 = (bf16[3,3,128,128]{3,2,1,0:T(8,128)(2,1)S(1)}, bf16[3,3,128,128]{3,2,1,0:T(8,128)(2,1)}, u32[]{:S(2)}) copy-start(bf16[3,3,128,128]{3,2,1,0:T(8,128)(2,1)} %param.20) | copy-start | bytes 884740
  5.7 1.0 %copy-start.5 = (bf16[3,3,128,128]{3,2,1,0:T(8,128)(2,1)S(1)}, bf16[3,3,128,128]{3,2,1,0:T(8,128)(2,1)}, u32[]{:S(2)}) copy-start(bf16[3,3,128,128]{3,2,1,0:T(8,128)(2,1)} %param.23) | copy-start | bytes 884740
  6.6 1.0 %copy-start.6 = (bf16[3,3,128,128]{3,2,1,0:T(8,128)(2,1)S(1)}, bf16[3,3,128,128]{3,2,1,0:T(8,128)(2,1)}, u32[]{:S(2)}) copy-start(bf16[3,3,128,128]{3,2,1,0:T(8,128)(2,1)} %param.24) | copy-start | bytes 884740
  7.6 1.0 %copy-start.7 = (bf16[3,3,128,128]{3,2,1,0:T(8,128)(2,1)S(1)}, bf16[3,3,128,128]{3,2,1,0:T(8,128)(2,1)}, u32[]{:S(2)}) copy-start(bf16[3,3,128,128]{3,2,1,0:T(8,128)(2,1)} %param.26) | copy-start | bytes 884740
  8.6 0.8 %copy-start.8 = (bf16[3,3,20,128]{3,2,1,0:T(8,128)(2,1)S(1)}, bf16[3,3,20,128]{3,2,1,0:T(8,128)(2,1)}, u32[]{:S(2)}) copy-start(bf16[3,3,20,128]{3,2,1,0:T(8,128)(2,1)} %refs_8_.1) | copy-start | bytes 138244
  9.4 0.8 %copy-start.9 = (bf16[3,3,12,128]{3,2,1,0:T(8,128)(2,1)S(1)}, bf16[3,3,12,128]{3,2,1,0:T(8,128)(2,1)}, u32[]{:S(2)}) copy-start(bf16[3,3,12,128]{3,2,1,0:T(8,128)(2,1)} %refs_2_.1) | copy-start | bytes 82948
  10.1 0.7 %copy-start.10 = (bf16[12,8,128]{2,1,0:T(8,128)(2,1)S(1)}, bf16[12,8,128]{2,1,0:T(8,128)(2,1)}, u32[]{:S(2)}) copy-start(bf16[12,8,128]{2,1,0:T(8,128)(2,1)} %refs_0_.1) | copy-start | bytes 73732
  10.9 0.7 %copy-start.11 = (f32[1,4,8,128]{3,2,1,0:T(8,128)S(1)}, f32[1,4,8,128]{3,2,1,0:T(8,128)}, u32[]{:S(2)}) copy-start(f32[1,4,8,128]{3,2,1,0:T(8,128)} %refs_1_.1) | copy-start | bytes 49156
  11.6 0.7 %copy-start.13 = (bf16[3,3,4,128]{3,2,1,0:T(4,128)(2,1)S(1)}, bf16[3,3,4,128]{3,2,1,0:T(4,128)(2,1)}, u32[]{:S(2)}) copy-start(bf16[3,3,4,128]{3,2,1,0:T(4,128)(2,1)} %refs_13_.1) | copy-start | bytes 27652

commit v2 on v1

--- a/solution.py
+++ b/solution.py
@@ -87,8 +87,9 @@
 
 
 def kernel(n, cols, *refs):
-    (cond_ref, noise_ref, rin_ref, rdown_h, rlow_h, rup_h, rfine_h, rout_ref,
-     din_ref, ddown_h, dlow_h, dup_h, dfine_h, dout_ref, out_ref,
+    (cond_h, noise_h, rin_h, rdown_h, rlow_h, rup_h, rfine_h, rout_h,
+     din_h, ddown_h, dlow_h, dup_h, dfine_h, dout_h, out_ref,
+     cond_ref, noise_ref, rin_ref, rout_ref, din_ref, dout_ref,
      rdown, rlow, rup, rfine, ddown, dlow, dup, dfine,
      rin, rall, din, dall,
      condb, noiseb, resb, fields, top, coarse, middle, joined, zbuf, mean, res,
@@ -103,6 +104,15 @@
              (ddown_h, ddown), (dlow_h, dlow), (dup_h, dup), (dfine_h, dfine)]
         )
     ]
+    small = [
+        pltpu.make_async_copy(src, dst, wsem.at[8 + i])
+        for i, (src, dst) in enumerate(
+            [(cond_h, cond_ref), (noise_h, noise_ref), (rin_h, rin_ref), (rout_h, rout_ref),
+             (din_h, din_ref), (dout_h, dout_ref)]
+        )
+    ]
+    for copy in small:
+        copy.start()
     offsets = [d for d in range(-REACH, REACH + 1) if d != 0]
 
     def there(d):
@@ -124,12 +134,14 @@
     m, k = iota2(shape, 0), iota2(shape, 1)
     gather = one_hot(k == (m % 16) * TILE + m // 16)
     gather = jnp.where(m % 16 < nch, gather.astype(F32), 0.0).astype(BF16)
+    small[0].wait()
     own = cond_ref[...].astype(F32).reshape(nch * TILE, cols).astype(BF16)
     own = dot(gather, dot(own, perm).astype(BF16)).astype(BF16)
     condb[REACH] = own.reshape(TILE, 16, cols)
     shape = (TILE * 8, 4 * TILE)
     m, k = iota2(shape, 0), iota2(shape, 1)
     pick = jnp.where((m % 8 < 4) & (k == (m % 8) * TILE + m // 8), 1.0, 0.0)
+    small[1].wait()
     noise = noise_ref[...].reshape(4 * TILE, cols)
     noise = jnp.dot(noise, perm_f, precision=HIGH, preferred_element_type=F32)
     noise = sigma_top * jnp.dot(pick, noise, precision=HIGH, preferred_element_type=F32)
@@ -185,6 +197,8 @@
         parts.append(jnp.zeros((8, ch), F32))
         dst[...] = jnp.concatenate(parts, axis=0).astype(BF16)
 
+    for copy in small[2:]:
+        copy.wait()
     place_in(rin_ref, rin, nch)
     place_out(rout_ref, rall, 4)
     place_in(din_ref, din, nch + 8)
@@ -216,7 +230,7 @@
             lax.fori_loop(0, count // chunk, step, 0)
 
         def do_top(r0):
-            c = 2
+            c = (span + 14) // 2
             parts = []
             for i in range(c):
                 parts.append(jnp.concatenate(
@@ -228,11 +242,11 @@
                 u = keep(v[i * cols : (i + 1) * cols], r0 + (i + lo - 7))
                 store_fine(top, r0 + i, u[:half], u[half:])
 
-        loop(span + 14, 2, do_top)
+        loop(span + 14, (span + 14) // 2, do_top)
         waits[0]()
 
         def do_coarse(r0):
-            c = 2
+            c = (span // 2 + 6) // 2
             lhs = jnp.concatenate(
                 [jnp.concatenate([top[2 * r0 + 2 * i + y, :half, :] for y in range(3)], axis=1)
                  for i in range(c)], axis=0)
@@ -241,11 +255,11 @@
                 u = keep(v[i * half : (i + 1) * half], 2 * r0 + (2 * i + lo - 6))
                 store_coarse(coarse, r0 + i, u)
 
-        loop(span // 2 + 6, 2, do_coarse)
+        loop(span // 2 + 6, (span // 2 + 6) // 2, do_coarse)
         waits[1]()
 
         def do_middle(r0):
-            c = 4
+            c = 8
             lhs = jnp.concatenate(
                 [coarse[pl.ds(r0 + y, c)].reshape(c * half, 3 * ch) for y in range(3)], axis=1)
             v = silu(dot(lhs, w_low[...]))
@@ -253,11 +267,11 @@
                 u = keep(v[i * half : (i + 1) * half], 2 * r0 + (2 * i + lo - 4))
                 store_coarse(middle, r0 + i, u)
 
-        loop(span // 2 + 4, 4, do_middle)
+        loop(span // 2 + 4, 8, do_middle)
         waits[2]()
 
         def do_joined(p0):
-            c = 2
+            c = (span // 2 + 2) // (2 if span > TILE else 1)
             rows = [middle[pl.ds(p0 + y, c)].reshape(c * half, 3 * ch) for y in range(3)]
             for ry, ((a, ka), (b, kb)) in enumerate((((0, 3), (1, 1)), ((1, 2), (2, 0)))):
                 sums = []
@@ -275,11 +289,11 @@
                     odd = keep(base[half:] + sums[1][i * half : (i + 1) * half], g)
                     store_fine(joined, t, even, odd)
 
-        loop(span // 2 + 2, 2, do_joined)
+        loop(span // 2 + 2, (span // 2 + 2) // (2 if span > TILE else 1), do_joined)
         waits[3]()
 
         def do_refined(r0):
-            c = 2
+            c = (span + 2) // 2
             lhs = jnp.concatenate(
                 [joined[pl.ds(r0 + y, c)].reshape(c * cols, 3 * ch) for y in range(3)], axis=1)
             v = silu(dot(lhs, w_fine[...]))
@@ -288,7 +302,7 @@
                 zbuf[r0 + i] = lax.dot_general(
                     w_all[...], u, (((1,), (1,)), ((), ())), preferred_element_type=F32)
 
-        loop(span + 2, 2, do_refined)
+        loop(span + 2, (span + 2) // 2, do_refined)
         sums = []
         for x in range(3):
             acc = None
@@ -368,9 +382,10 @@
     return pl.pallas_call(
         functools.partial(kernel, n, cols),
         out_shape=jax.ShapeDtypeStruct(noise.shape, F32),
-        in_specs=[vm, vm, vm, hb, hb, hb, hb, vm, vm, hb, hb, hb, hb, vm],
+        in_specs=[hb] * 14,
         out_specs=vm,
         scratch_shapes=[
+            *[pltpu.VMEM(a.shape, a.dtype) for a in (cond, noise, rin, rout, din, dout)],
             *[pltpu.VMEM(s, BF16) for s in (big, big, (16, ch, ch), big) * 2],
             pltpu.VMEM((240, ch), BF16),
             pltpu.VMEM((80, ch), BF16),
@@ -387,10 +402,10 @@
             pltpu.VMEM((wide + 2, 80, cols), F32),
             pltpu.VMEM((3, TILE * 8, cols), F32),
             pltpu.VMEM((TILE * 8, cols), F32),
-            dma((8,)), dma((5,)), dma((5,)), dma((3,)), dma((3,)), dma((3,)), dma((3,)),
+            dma((14,)), dma((5,)), dma((5,)), dma((3,)), dma((3,)), dma((3,)), dma((3,)),
         ],
         compiler_params=pltpu.CompilerParams(
-            collective_id=0, has_side_effects=True, vmem_limit_bytes=48 * 1024 * 1024
+            collective_id=0, has_side_effects=True, vmem_limit_bytes=64 * 1024 * 1024
         ),
         cost_estimate=pl.CostEstimate(flops=4 * 10**9, bytes_accessed=3 * 10**6, transcendentals=2 * 10**6),
     )(cond, noise, rin, flat(rdown), flat(rlow), taps(rup), flat(rfine), rout,

time: 57.2 us -> 31.3 us (0.55)
  Pallas kernels: 43.6 us -> 29.7 us
  local copies, waits for them, and re-layouts: 12.9 us -> 1.32 us
    pallas_call x1, Pallas kernels: 43.6 us -> 29.7 us  [shards(): pl.pallas_call(functools.partial(kernel, n, cols), out_shape=jax.ShapeDty...]
    unnamed x29 -> x1, local copies, waits for them, and re-layouts: 12.9 us -> 1.32 us
where the time goes in v2:
time: 31.3 us; the launch traced here: 31 us
  Pallas kernels  29.7 us (95%)
  local copies, waits for them, and re-layouts  1.32 us (4%)
    pallas_call x1, Pallas kernels, shards(): pl.pallas_call(functools.partial(kernel, n, cols), out_shape=jax.ShapeDty...  29.7 us
    unnamed x1, local copies, waits for them, and re-layouts  1.32 us

profile of v2, /device:TPU:3, one launch (start us, length us, event | category | flops | bytes accessed | tf_op | source)
XLA Modules:
  0.0 31.0 jit_solution(11012609553086678322)
XLA Ops:
  0.0 29.7 %shard_map.136 = f32[1,4,8,128]{3,2,1,0:T(8,128)} custom-call(bf16[12,8,128]{2,1,0:T(8,128)(2,1)} %refs_0_.1, f32[1,4,8,128]{3,2,1,0:T(8,128)} %refs_1_.1, bf16[3,3,12,128]{3,2,1,0:T(8,128)(2,1)} %refs_2_.1, bf16[1152,128]{1,0:T(8,128)(2,1)} %bitcast.10, bf16[1152,128]{1,0:T(8,128)(2,1)} %bitcast.11, bf16[16,128,128]{2,1,0:T(8,128)(2,1)} %bitcast.8, ...), custom_call_target="tpu_custom_call" | custom-call | flops 4000000000 | bytes 3000000 | tf_op jit(solution)/shard_map/pallas_call | solution.py:382
  29.7 1.3 %copy.16 = f32[1,4,8,128]{3,2,1,0:T(8,128)} copy(f32[1,4,8,128]{3,2,1,0:T(8,128)} %shard_map.136) | data formatting | bytes 32768

commit v3 on v2

--- a/solution.py
+++ b/solution.py
@@ -17,6 +17,7 @@
 HIGH = lax.Precision.HIGHEST
 TILE = 8
 REACH = 2
+PARTS = 4
 
 
 def step_gains(k):
@@ -93,8 +94,11 @@
      rdown, rlow, rup, rfine, ddown, dlow, dup, dfine,
      rin, rall, din, dall,
      condb, noiseb, resb, fields, top, coarse, middle, joined, zbuf, mean, res,
-     wsem, csend, crecv, nsend, nrecv, rsend, rrecv) = refs
+     meanb, wsem, csend, crecv, nsend, nrecv, rsend, rrecv, msend, mrecv) = refs
     me = lax.axis_index("tile")
+    member = lax.axis_index("ens")
+    part = member % PARTS
+    rows_each = 3 * TILE // PARTS
     half = cols // 2
     ch = 128
     loads = [
@@ -124,6 +128,10 @@
         def _():
             pl.semaphore_signal(barrier, inc=1, device_id={"tile": me + d},
                                 device_id_type=pl.DeviceIdType.MESH)
+    for j in range(1, PARTS):
+        pl.semaphore_signal(barrier, inc=1,
+                            device_id={"ens": member - part + (part + j) % PARTS},
+                            device_id_type=pl.DeviceIdType.MESH)
     for copy in loads:
         copy.start()
 
@@ -155,7 +163,7 @@
                 noiseb[1 + d] = jnp.zeros_like(noiseb[1 + d])
                 resb[1 + d] = jnp.zeros_like(resb[1 + d])
 
-    pl.semaphore_wait(barrier, jnp.minimum(me, REACH) + jnp.minimum(n - 1 - me, REACH))
+    pl.semaphore_wait(barrier, jnp.minimum(me, REACH) + jnp.minimum(n - 1 - me, REACH) + (PARTS - 1))
 
     def cond_copy(d, incoming=False):
         return pltpu.make_async_remote_copy(
@@ -214,8 +222,7 @@
         at = (REACH + d) * TILE
         fields[at : at + TILE] = both
 
-    def unet(lo, hi, w_in, w_down, w_low, w_up, w_fine, w_all, waits):
-        span = hi - lo
+    def unet(lo, span, w_in, w_down, w_low, w_up, w_fine, w_all, waits):
         first = me * TILE
         last = n * TILE
 
@@ -246,7 +253,7 @@
         waits[0]()
 
         def do_coarse(r0):
-            c = (span // 2 + 6) // 2
+            c = span // 2 + 6
             lhs = jnp.concatenate(
                 [jnp.concatenate([top[2 * r0 + 2 * i + y, :half, :] for y in range(3)], axis=1)
                  for i in range(c)], axis=0)
@@ -255,11 +262,11 @@
                 u = keep(v[i * half : (i + 1) * half], 2 * r0 + (2 * i + lo - 6))
                 store_coarse(coarse, r0 + i, u)
 
-        loop(span // 2 + 6, (span // 2 + 6) // 2, do_coarse)
+        loop(span // 2 + 6, span // 2 + 6, do_coarse)
         waits[1]()
 
         def do_middle(r0):
-            c = 8
+            c = span // 2 + 4
             lhs = jnp.concatenate(
                 [coarse[pl.ds(r0 + y, c)].reshape(c * half, 3 * ch) for y in range(3)], axis=1)
             v = silu(dot(lhs, w_low[...]))
@@ -267,11 +274,11 @@
                 u = keep(v[i * half : (i + 1) * half], 2 * r0 + (2 * i + lo - 4))
                 store_coarse(middle, r0 + i, u)
 
-        loop(span // 2 + 4, 8, do_middle)
+        loop(span // 2 + 4, span // 2 + 4, do_middle)
         waits[2]()
 
         def do_joined(p0):
-            c = (span // 2 + 2) // (2 if span > TILE else 1)
+            c = span // 2 + 2
             rows = [middle[pl.ds(p0 + y, c)].reshape(c * half, 3 * ch) for y in range(3)]
             for ry, ((a, ka), (b, kb)) in enumerate((((0, 3), (1, 1)), ((1, 2), (2, 0)))):
                 sums = []
@@ -289,7 +296,7 @@
                     odd = keep(base[half:] + sums[1][i * half : (i + 1) * half], g)
                     store_fine(joined, t, even, odd)
 
-        loop(span // 2 + 2, (span // 2 + 2) // (2 if span > TILE else 1), do_joined)
+        loop(span // 2 + 2, span // 2 + 2, do_joined)
         waits[3]()
 
         def do_refined(r0):
@@ -297,10 +304,13 @@
             lhs = jnp.concatenate(
                 [joined[pl.ds(r0 + y, c)].reshape(c * cols, 3 * ch) for y in range(3)], axis=1)
             v = silu(dot(lhs, w_fine[...]))
+            u = jnp.concatenate(
+                [keep(v[i * cols : (i + 1) * cols], r0 + (i + lo - 1)).astype(BF16)
+                 for i in range(c)], axis=0)
+            z = lax.dot_general(
+                w_all[...], u, (((1,), (1,)), ((), ())), preferred_element_type=F32)
             for i in range(c):
-                u = keep(v[i * cols : (i + 1) * cols], r0 + (i + lo - 1)).astype(BF16)
-                zbuf[r0 + i] = lax.dot_general(
-                    w_all[...], u, (((1,), (1,)), ((), ())), preferred_element_type=F32)
+                zbuf[r0 + i] = z[:, i * cols : (i + 1) * cols]
 
         loop(span + 2, (span + 2) // 2, do_refined)
         sums = []
@@ -319,11 +329,25 @@
             cond_copy(d, True).wait_recv()
     for d in range(-REACH, REACH + 1):
         put_fields(d, jnp.zeros((TILE, 8, cols), F32))
-    value = unet(-TILE, 2 * TILE, rin, rdown, rlow, rup, rfine, rall,
+    value = unet(part * rows_each - TILE, rows_each, rin, rdown, rlow, rup, rfine, rall,
                  [c.wait for c in loads[:4]])
+    meanb[part] = value
+
+    def mean_copy(j, incoming=False):
+        slot = (part + PARTS - j) % PARTS if incoming else part
+        return pltpu.make_async_remote_copy(
+            src_ref=meanb.at[part], dst_ref=meanb.at[slot],
+            send_sem=msend.at[j], recv_sem=mrecv.at[j],
+            device_id={"ens": member - part + (part + j) % PARTS},
+            device_id_type=pl.DeviceIdType.MESH)
+
+    for j in range(1, PARTS):
+        mean_copy(j).start()
+    for j in range(1, PARTS):
+        mean_copy(j, True).wait_recv()
+    value = meanb[...].reshape(3 * TILE * 8, cols)
     for d in (-1, 0, 1):
-        part = value[(d + 1) * 64 : (d + 2) * 64]
-        mean[d + 1] = jnp.where(there(d), part, 0.0)
+        mean[d + 1] = jnp.where(there(d), value[(d + 1) * TILE * 8 : (d + 2) * TILE * 8], 0.0)
 
     nothing = lambda: None
     for step in range(STEPS):
@@ -356,6 +380,8 @@
                             preferred_element_type=F32)
     out_ref[...] = total.reshape(1, 4, TILE, cols)
 
+    for j in range(1, PARTS):
+        mean_copy(j).wait_send()
     for d in offsets:
         @pl.when(there(d))
         def _():
@@ -377,7 +403,8 @@
     vm = pl.BlockSpec(memory_space=pltpu.VMEM)
     hb = pl.BlockSpec(memory_space=pl.ANY)
     big = (9 * ch, ch)
-    wide = 3 * TILE
+    assert lax.axis_size("ens") % PARTS == 0
+    wide = TILE
     dma = pltpu.SemaphoreType.DMA
     return pl.pallas_call(
         functools.partial(kernel, n, cols),
@@ -402,7 +429,9 @@
             pltpu.VMEM((wide + 2, 80, cols), F32),
             pltpu.VMEM((3, TILE * 8, cols), F32),
             pltpu.VMEM((TILE * 8, cols), F32),
+            pltpu.VMEM((PARTS, 3 * TILE // PARTS * 8, cols), F32),
             dma((14,)), dma((5,)), dma((5,)), dma((3,)), dma((3,)), dma((3,)), dma((3,)),
+            dma((PARTS,)), dma((PARTS,)),
         ],
         compiler_params=pltpu.CompilerParams(
             collective_id=0, has_side_effects=True, vmem_limit_bytes=64 * 1024 * 1024

time: 31.3 us -> 32.3 us (1.032)
  Pallas kernels: 29.7 us -> 30.6 us
    pallas_call x1, Pallas kernels: 29.7 us -> 30.6 us  [shards(): pl.pallas_call(functools.partial(kernel, n, cols), out_shape=jax.ShapeDty...]
where the time goes in v3:
time: 32.3 us; the launch traced here: 31.9 us
  Pallas kernels  30.6 us (95%)
  local copies, waits for them, and re-layouts  1.32 us (4%)
    pallas_call x1, Pallas kernels, shards(): pl.pallas_call(functools.partial(kernel, n, cols), out_shape=jax.ShapeDty...  30.6 us
    unnamed x1, local copies, waits for them, and re-layouts  1.32 us

profile of v3, /device:TPU:3, one launch (start us, length us, event | category | flops | bytes accessed | tf_op | source)
XLA Modules:
  0.0 31.9 jit_solution(16396221044668522614)
XLA Ops:
  0.0 30.6 %shard_map.136 = f32[1,4,8,128]{3,2,1,0:T(8,128)} custom-call(bf16[12,8,128]{2,1,0:T(8,128)(2,1)} %refs_0_.1, f32[1,4,8,128]{3,2,1,0:T(8,128)} %refs_1_.1, bf16[3,3,12,128]{3,2,1,0:T(8,128)(2,1)} %refs_2_.1, bf16[1152,128]{1,0:T(8,128)(2,1)} %bitcast.10, bf16[1152,128]{1,0:T(8,128)(2,1)} %bitcast.11, bf16[16,128,128]{2,1,0:T(8,128)(2,1)} %bitcast.8, ...), custom_call_target="tpu_custom_call" | custom-call | flops 4000000000 | bytes 3000000 | tf_op jit(solution)/shard_map/pallas_call | solution.py:409
  30.6 1.3 %copy.16 = f32[1,4,8,128]{3,2,1,0:T(8,128)} copy(f32[1,4,8,128]{3,2,1,0:T(8,128)} %shard_map.136) | data formatting | bytes 32768

commit v4 on v2

--- a/solution.py
+++ b/solution.py
@@ -97,11 +97,18 @@
     me = lax.axis_index("tile")
     half = cols // 2
     ch = 128
+    for w in (rfine, dfine):
+        w[9 * ch :, :ch] = jnp.zeros((3 * ch, ch), BF16)
+        w[: 3 * ch, ch:] = jnp.zeros((3 * ch, ch), BF16)
+    seconds = [
+        pltpu.make_async_copy(src, dst.at[3 * ch :, ch:], wsem.at[14 + i])
+        for i, (src, dst) in enumerate([(rfine_h, rfine), (dfine_h, dfine)])
+    ]
     loads = [
         pltpu.make_async_copy(src, dst, wsem.at[i])
         for i, (src, dst) in enumerate(
-            [(rdown_h, rdown), (rlow_h, rlow), (rup_h, rup), (rfine_h, rfine),
-             (ddown_h, ddown), (dlow_h, dlow), (dup_h, dup), (dfine_h, dfine)]
+            [(rdown_h, rdown), (rlow_h, rlow), (rup_h, rup), (rfine_h, rfine.at[: 9 * ch, :ch]),
+             (ddown_h, ddown), (dlow_h, dlow), (dup_h, dup), (dfine_h, dfine.at[: 9 * ch, :ch])]
         )
     ]
     small = [
@@ -124,7 +131,7 @@
         def _():
             pl.semaphore_signal(barrier, inc=1, device_id={"tile": me + d},
                                 device_id_type=pl.DeviceIdType.MESH)
-    for copy in loads:
+    for copy in loads + seconds:
         copy.start()
 
     perm = one_hot(iota2((cols, cols), 0) == 2 * (iota2((cols, cols), 1) % half) + iota2((cols, cols), 1) // half)
@@ -291,18 +298,21 @@
 
         loop(span // 2 + 2, (span // 2 + 2) // (2 if span > TILE else 1), do_joined)
         waits[3]()
+        waits[4]()
 
         def do_refined(r0):
-            c = (span + 2) // 2
+            c = span + 2
             lhs = jnp.concatenate(
-                [joined[pl.ds(r0 + y, c)].reshape(c * cols, 3 * ch) for y in range(3)], axis=1)
+                [jnp.concatenate([joined[r0 + (2 * i + y)] for i in range(c // 2)], axis=0)
+                 for y in range(4)], axis=1)
             v = silu(dot(lhs, w_fine[...]))
             for i in range(c):
-                u = keep(v[i * cols : (i + 1) * cols], r0 + (i + lo - 1)).astype(BF16)
+                u = v[i // 2 * cols : (i // 2 + 1) * cols, i % 2 * ch : (i % 2 + 1) * ch]
+                u = keep(u, r0 + (i + lo - 1)).astype(BF16)
                 zbuf[r0 + i] = lax.dot_general(
                     w_all[...], u, (((1,), (1,)), ((), ())), preferred_element_type=F32)
 
-        loop(span + 2, (span + 2) // 2, do_refined)
+        loop(span + 2, span + 2, do_refined)
         sums = []
         for x in range(3):
             acc = None
@@ -320,7 +330,7 @@
     for d in range(-REACH, REACH + 1):
         put_fields(d, jnp.zeros((TILE, 8, cols), F32))
     value = unet(-TILE, 2 * TILE, rin, rdown, rlow, rup, rfine, rall,
-                 [c.wait for c in loads[:4]])
+                 [c.wait for c in loads[:4]] + [seconds[0].wait])
     for d in (-1, 0, 1):
         part = value[(d + 1) * 64 : (d + 2) * 64]
         mean[d + 1] = jnp.where(there(d), part, 0.0)
@@ -336,7 +346,7 @@
         for d in (-1, 0, 1):
             put_fields(d, (buf[1 + d].astype(F32) + mean[1 + d]).reshape(TILE, 8, cols))
         net = unet(0, TILE, din, ddown, dlow, dup, dfine, dall,
-                   [c.wait for c in loads[4:]] if step == 0 else [nothing] * 4)
+                   [c.wait for c in loads[4:]] + [seconds[1].wait] if step == 0 else [nothing] * 5)
         now = res[...]
         now = now + rate * (now - (skip * now + gain * net))
         if step + 1 < STEPS:
@@ -386,7 +396,7 @@
         out_specs=vm,
         scratch_shapes=[
             *[pltpu.VMEM(a.shape, a.dtype) for a in (cond, noise, rin, rout, din, dout)],
-            *[pltpu.VMEM(s, BF16) for s in (big, big, (16, ch, ch), big) * 2],
+            *[pltpu.VMEM(s, BF16) for s in (big, big, (16, ch, ch), (12 * ch, 2 * ch)) * 2],
             pltpu.VMEM((240, ch), BF16),
             pltpu.VMEM((80, ch), BF16),
             pltpu.VMEM((240, ch), BF16),
@@ -402,7 +412,7 @@
             pltpu.VMEM((wide + 2, 80, cols), F32),
             pltpu.VMEM((3, TILE * 8, cols), F32),
             pltpu.VMEM((TILE * 8, cols), F32),
-            dma((14,)), dma((5,)), dma((5,)), dma((3,)), dma((3,)), dma((3,)), dma((3,)),
+            dma((16,)), dma((5,)), dma((5,)), dma((3,)), dma((3,)), dma((3,)), dma((3,)),
         ],
         compiler_params=pltpu.CompilerParams(
             collective_id=0, has_side_effects=True, vmem_limit_bytes=64 * 1024 * 1024

time: 31.3 us -> 29.9 us (0.955)
  Pallas kernels: 29.7 us -> 28.3 us
    pallas_call x1, Pallas kernels: 29.7 us -> 28.3 us  [shards(): pl.pallas_call(functools.partial(kernel, n, cols), out_shape=jax.ShapeDty...]
where the time goes in v4:
time: 29.9 us; the launch traced here: 29.7 us
  Pallas kernels  28.3 us (95%)
  local copies, waits for them, and re-layouts  1.32 us (4%)
    pallas_call x1, Pallas kernels, shards(): pl.pallas_call(functools.partial(kernel, n, cols), out_shape=jax.ShapeDty...  28.3 us
    unnamed x1, local copies, waits for them, and re-layouts  1.32 us

profile of v4, /device:TPU:3, one launch (start us, length us, event | category | flops | bytes accessed | tf_op | source)
XLA Modules:
  0.0 29.7 jit_solution(3719919104153665715)
XLA Ops:
  0.0 28.3 %shard_map.136 = f32[1,4,8,128]{3,2,1,0:T(8,128)} custom-call(bf16[12,8,128]{2,1,0:T(8,128)(2,1)} %refs_0_.1, f32[1,4,8,128]{3,2,1,0:T(8,128)} %refs_1_.1, bf16[3,3,12,128]{3,2,1,0:T(8,128)(2,1)} %refs_2_.1, bf16[1152,128]{1,0:T(8,128)(2,1)} %bitcast.10, bf16[1152,128]{1,0:T(8,128)(2,1)} %bitcast.11, bf16[16,128,128]{2,1,0:T(8,128)(2,1)} %bitcast.8, ...), custom_call_target="tpu_custom_call" | custom-call | flops 4000000000 | bytes 3000000 | tf_op jit(solution)/shard_map/pallas_call | solution.py:392
  28.3 1.3 %copy.16 = f32[1,4,8,128]{3,2,1,0:T(8,128)} copy(f32[1,4,8,128]{3,2,1,0:T(8,128)} %shard_map.136) | data formatting | bytes 32768
